TPU v7x, 256 devices: a whole 4x4x8 slice. The times are simulated.
256 devices in a mesh: dp: 32 (over z_lo, y, core), tensor: 8 (over z_hi, x).
Axes of the slice: x: 4, y: 4, z: 8 (z_hi: 2, z_lo: 4; z = z_hi * 4 + z_lo), core: 2. Of those that a mesh axis runs over, the one named last changes fastest.
Arguments:
- tokens: bfloat16 [12288, 2560], P(('dp', 'tensor')), may hold values from -24 to 24
- cotangent: bfloat16 [12288, 2560], P(('dp', 'tensor')), may hold values from -1280 to 1280
- gate_pre: bfloat16 [12288, 9216], P('dp', 'tensor'), may hold values from -8 to 8
- up_pre: bfloat16 [12288, 9216], P('dp', 'tensor'), may hold values from -6 to 6
- down_weight: bfloat16 [2560, 9216], P('dp', 'tensor'), may hold values from -0.0625 to 0.0625
- counts: int32 [32, 8], P('dp'), may hold values from 8 to 48, as said below
Outputs:
- grad_gate: float32 [2560, 9216], P('dp', 'tensor')
- grad_up: float32 [2560, 9216], P('dp', 'tensor')
Inputs may be any that keep to these rules, and one draw needn't show every extreme that they name: `counts`: every count is a multiple of 8.
All inputs are finite; a program needn't handle non-finite values.
Results may differ from a plain program's by a relative error of at most 0.0029.
Values may be sent and summed in bfloat16 or wider, within the bound.
No kernel may reach another device: no remote copies, remote signals or barrier semaphores. Data moves between devices by JAX's collectives and lax.ppermute only.
A program may use at most 128 MiB of HBM per device.

v0:
```python
import jax
import jax.numpy as jnp
from jax import lax
from jax.sharding import PartitionSpec as P

MB_SLOTS = 48


def rows_product(left, right, inverse):
    product = lax.dot_general(
        left, right, (((0,), (0,)), ((), ())), preferred_element_type=jnp.float32
    )
    return product * inverse


def local(tokens, cotangent, gate_pre, up_pre, down_weight, counts):
    own_total = jnp.sum(counts).astype(jnp.float32)
    total = lax.psum(own_total, "dp")
    inverse = 1.0 / total
    slot_index = jnp.arange(MB_SLOTS, dtype=jnp.int32)
    valid_slot = (slot_index[None, :] < counts[0][:, None]).reshape(-1)
    whole_tokens, whole_grads = (
        lax.all_gather(tokens, "tensor", axis=0, tiled=True),
        lax.all_gather(cotangent, "tensor", axis=0, tiled=True),
    )
    masked = jnp.where(valid_slot[:, None], whole_grads, jnp.zeros_like(whole_grads))
    hidden_grad = jnp.dot(
        masked,
        lax.all_gather(down_weight, "dp", axis=0, tiled=True),
        preferred_element_type=jnp.float32,
    )
    gate_value = gate_pre.astype(jnp.float32)
    up_value = up_pre.astype(jnp.float32)
    sigmoid_gate = jax.nn.sigmoid(gate_value)
    gate_delta = (
        hidden_grad * up_value * sigmoid_gate * (1.0 + gate_value * (1.0 - sigmoid_gate))
    ).astype(jnp.bfloat16)
    up_delta = (hidden_grad * gate_value * sigmoid_gate).astype(jnp.bfloat16)
    term_gate = rows_product(whole_tokens, gate_delta, inverse)
    term_up = rows_product(whole_tokens, up_delta, inverse)
    grad_gate, grad_up = (
        lax.psum_scatter(term_gate, "dp", scatter_dimension=0, tiled=True),
        lax.psum_scatter(term_up, "dp", scatter_dimension=0, tiled=True),
    )
    return (grad_gate, grad_up)


def solution(mesh):
    placed = (
        P(("dp", "tensor"), None),
        P(("dp", "tensor"), None),
        P("dp", "tensor"),
        P("dp", "tensor"),
        P("dp", "tensor"),
        P("dp", None),
    )
    return jax.shard_map(
        local,
        mesh=mesh,
        in_specs=placed,
        out_specs=(P("dp", "tensor"), P("dp", "tensor")),
        check_vma=False,
    )
```

profile of v0, /device:TPU:4, one launch (start us, length us, event | category | flops | bytes accessed | tf_op | source)
XLA Modules:
  0.0 579.4 jit_solution(11819870697249910660)
XLA Ops:
  7.2 0.0 all-gather.4.cloned.1.call-start
  7.2 0.7 all-gather.4.cloned.1.call-update
  7.9 0.0 all-gather.6.cloned.1.call-start
  7.9 0.7 all-gather.6.cloned.1.call-update
  8.6 0.0 all-gather.8.cloned.1.call-start
  8.7 0.7 all-gather.8.cloned.1.call-update
  9.4 0.0 reduce-scatter.9.cloned.1.call-start
  9.4 1.3 reduce_sum.9
  11.4 76.9 %psum.7 = f32[]{:T(128)} all-reduce(f32[]{:T(128)S(6)} %convert_element_type.18), channel_id=1, replica_groups=mesh['dp'=32,'tensor'=8] {'dp'}, use_global_device_ids=true, to_apply=%region_1.0 | all-reduce | flops 1 | bytes 8 | tf_op jit(solution)/shard_map/psum | solution.py:18
  88.3 0.7 iota_compare_fusion
  89.0 0.1 lt.26
  89.8 0.0 all-gather.4.cloned.1.call-done
  89.8 61.4 %all-gather.6.cloned.1.call-done = bf16[2560,1152]{1,0:T(8,128)(2,1)} async-done(((bf16[80,1152]{1,0:T(8,128)(2,1)}), bf16[2560,1152]{1,0:T(8,128)(2,1)}) %all-gather.6.cloned.1.call-update) | async-done | bytes 5898256 | tf_op jit(solution)/shard_map/all_gather | solution.py:29
  151.3 6.0 %fusion.2 = f32[384,1152]{1,0:T(8,128)S(1)} fusion(bf16[2560,1152]{1,0:T(8,128)(2,1)} %all-gather.6.cloned.1.call-done, bf16[384,2560]{1,0:T(8,128)(2,1)} %all-gather.4.cloned.1.call-done, pred[384]{0:T(512)(128)(4,1)S(1)} %lt.26), kind=kOutput, calls=%fused_computation.7 | convolution fusion | flops 2265907200 | bytes 9634176 | tf_op jit(solution)/shard_map/dot_general | solution.py:27
  157.3 68.8 %all-gather.8.cloned.1.call-done = bf16[384,2560]{1,0:T(8,128)(2,1)} async-done(((bf16[48,2560]{1,0:T(8,128)(2,1)}), bf16[384,2560]{1,0:T(8,128)(2,1)}) %all-gather.8.cloned.1.call-update) | async-done | bytes 1966096 | tf_op jit(solution)/shard_map/all_gather | solution.py:23
  226.1 9.1 %fusion.1 = f32[2560,1152]{0,1:T(8,128)} fusion(bf16[384,2560]{1,0:T(8,128)(2,1)} %all-gather.8.cloned.1.call-done, f32[]{:T(128)S(6)} %div.7, f32[384,1152]{1,0:T(8,128)S(1)} %fusion.2, bf16[384,1152]{1,0:T(8,128)(2,1)S(1)} %copy-done.1), kind=kOutput, calls=%fused_computation.3 | convolution fusion | flops 2270969856 | bytes 16416772 | tf_op jit(solution)/shard_map/dot_general | solution.py:10
  235.3 13.6 %copy.14 = f32[2560,1152]{1,0:T(8,128)} copy(f32[2560,1152]{0,1:T(8,128)} %fusion.1) | data formatting | bytes 23592960
  248.9 0.0 reduce-scatter.9.cloned.1.call-update
  248.9 0.0 reduce-scatter.7.cloned.1.call-start
  249.0 1.5 copy-done
  250.4 8.4 %fusion = f32[2560,1152]{0,1:T(8,128)} fusion(bf16[384,2560]{1,0:T(8,128)(2,1)S(1)} %copy-done, f32[]{:T(128)S(6)} %div.7, bf16[384,1152]{1,0:T(8,128)(2,1)S(1)} %copy-done.1, f32[384,1152]{1,0:T(8,128)} %copy-done.2, bf16[384,1152]{1,0:T(8,128)(2,1)} %param.9), kind=kOutput, calls=%fused_computation.2 | convolution fusion | flops 2273181696 | bytes 17301508 | tf_op jit(solution)/shard_map/dot_general | solution.py:10
  258.9 13.5 %copy.12 = f32[2560,1152]{1,0:T(8,128)} copy(f32[2560,1152]{0,1:T(8,128)} %fusion) | data formatting | bytes 23592960
  272.4 137.4 %reduce-scatter.9.cloned.1.call-done = f32[80,1152]{1,0:T(8,128)} async-done(((f32[2560,1152]{1,0:T(8,128)}), f32[80,1152]{1,0:T(8,128)}) %reduce-scatter.9.cloned.1.call-update) | async-done | bytes 368656
  409.8 163.0 %reduce-scatter.7.cloned.1.call-done = f32[80,1152]{1,0:T(8,128)} async-done(((f32[2560,1152]{1,0:T(8,128)}), f32[80,1152]{1,0:T(8,128)}) %reduce-scatter.7.cloned.1.call-update) | async-done | bytes 368656
  (6 shorter events, 0.0 us)
Async XLA Ops:
  7.2 82.7 %all-gather.4.cloned.1.call-start = ((), (), s32[]{:S(2)}) async-start(), calls=%async_computation.2 | async-start | bytes 2211840 | tf_op jit(solution)/shard_map/all_gather | solution.py:24
  7.9 143.4 %all-gather.6.cloned.1.call-start = ((), (), s32[]{:S(2)}) async-start(), calls=%async_computation.3 | async-start | bytes 6082560 | tf_op jit(solution)/shard_map/all_gather | solution.py:29
  8.6 217.5 %all-gather.8.cloned.1.call-start = ((), (), s32[]{:S(2)}) async-start(), calls=%async_computation.4 | async-start | bytes 2211840 | tf_op jit(solution)/shard_map/all_gather | solution.py:23
  9.4 400.4 %reduce-scatter.9.cloned.1.call-start = ((), (), s32[]{:S(2)}) async-start(), calls=%async_computation.6 | async-start | bytes 12165120
  89.8 136.3 %copy-start.1 = (bf16[384,1152]{1,0:T(8,128)(2,1)S(1)}, bf16[384,1152]{1,0:T(8,128)(2,1)}, u32[]{:S(2)}) copy-start(bf16[384,1152]{1,0:T(8,128)(2,1)} %param.8) | copy-start | bytes 2654212
  157.3 78.0 %copy-start.2 = (f32[384,1152]{1,0:T(8,128)}, f32[384,1152]{1,0:T(8,128)S(1)}, u32[]{:S(2)}) copy-start(f32[384,1152]{1,0:T(8,128)S(1)} %fusion.2) | copy-start | bytes 5308420
  248.9 1.5 copy-start
  248.9 323.9 %reduce-scatter.7.cloned.1.call-start = ((), (), s32[]{:S(2)}) async-start(), calls=%async_computation.5 | async-start | bytes 12165120
Sparse Core Ops, SparseCore 0:
  10.6 76.0 all-gather.3
  88.5 62.7 all-gather.5
  153.9 72.2 all-gather.7
  249.0 160.7 reduce-scatter.8
  413.0 159.8 reduce-scatter.6
where the time goes:
time: 580 us; the launch traced here: 579 us
  waiting for transfers between devices  433 us (75%)
  blocking collectives  76.9 us (13%)
  local copies, waits for them, and re-layouts  28.7 us (5%)
  matrix products  23.6 us (4%)
  between operations  15.2 us (3%)
    unnamed x7, waiting for transfers between devices  303 us
    psum x1, blocking collectives, local(): total = lax.psum(own_total, 'dp')  76.9 us
    all_gather x1, waiting for transfers between devices, local(): lax.all_gather(tokens, 'tensor', axis=0, tiled=True)  68.8 us
    all_gather x1, waiting for transfers between devices, local(): lax.all_gather(down_weight, 'dp', axis=0, tiled=True)  61.4 us
    unnamed x8, local copies, waits for them, and re-layouts  28.6 us
    dot_general x2, matrix products, rows_product(): lax.dot_general(left, right, (((0,), (0,)), ((), ())), preferred_element_...  17.6 us
  transfers between devices with their start and end apart: 5, of which 4 were waited for; matrix products, arithmetic and copies ran while one was open for 5% of the time, Pallas kernels for 0%

commit v1 on v0

v1 whole, which is shorter than its diff:
```python
import jax
import jax.numpy as jnp
from jax import lax
from jax.experimental import pallas as pl
from jax.experimental.pallas import tpu as pltpu
from jax.sharding import PartitionSpec as P

NZ, NY, NC, NW, NX = 4, 4, 2, 2, 4
SLOTS = 48
BLK = 80
D = BLK * NZ * NY * NC
HALF = D // 2
QUART = D // 4
FF = 1152
ROWS = SLOTS * NW * NX
bf16, f32 = jnp.bfloat16, jnp.float32
def dp_move(x, fn):
    pairs = []
    for z in range(NZ):
        for y in range(NY):
            for c in range(NC):
                tz, ty, tc = fn(z, y, c)
                pairs.append(((z * NY + y) * NC + c, (tz * NY + ty) * NC + tc))
    return lax.ppermute(x, "dp", pairs)


def tp_move(x, fn):
    pairs = []
    for w in range(NW):
        for k in range(NX):
            tw, tk = fn(w, k)
            pairs.append((w * NX + k, tw * NX + tk))
    return lax.ppermute(x, "tensor", pairs)


def GATE_PAIR(z, y, c):
    return z, y ^ 1, c


def UP_PAIR(z, y, c):
    return z, 3 - y, c


def core_swap(x):
    return dp_move(x, lambda z, y, c: (z, y, 1 - c))


def vmem():
    return pl.BlockSpec(memory_space=pltpu.VMEM)


def smem():
    return pl.BlockSpec(memory_space=pltpu.SMEM)


def call(body, out_shape, n_smem, n_vmem, scratch=(), flops=0, nbytes=0, mb=40):
    return pl.pallas_call(
        body,
        out_shape=out_shape,
        in_specs=[smem()] * n_smem + [vmem()] * n_vmem,
        out_specs=jax.tree.map(lambda _: vmem(), out_shape),
        scratch_shapes=list(scratch),
        compiler_params=pltpu.CompilerParams(vmem_limit_bytes=mb << 20),
        cost_estimate=pl.CostEstimate(flops=flops, bytes_accessed=nbytes, transcendentals=0),
    )


def sds(shape, dtype):
    return jax.ShapeDtypeStruct(shape, dtype)


def columns(x, chosen):
    return jnp.concatenate([x[:, i * BLK : (i + 1) * BLK] for i in chosen], axis=1)


def half_blocks(core):
    return [chip * NC + core for chip in range(NZ * NY)]


def split_body(pos, counts, cot, tok, keep, send):
    live = counts[0, pos[3] * NX + pos[4]]
    row = lax.broadcasted_iota(jnp.int32, (SLOTS, 1), 0)
    first = pos[2] == 0
    cot_rows = jnp.where(row < live, cot[...].astype(f32), 0.0)
    for at, x in ((0, cot_rows), (SLOTS, tok[...].astype(f32))):
        even, odd = columns(x, half_blocks(0)), columns(x, half_blocks(1))
        keep[at : at + SLOTS, :] = jnp.where(first, even, odd).astype(bf16)
        send[at : at + SLOTS, :] = jnp.where(first, odd, even).astype(bf16)
    total = counts[0, 0]
    for m in range(1, 8):
        total += counts[0, m]
    eighths = jnp.full((16, HALF), lax.div(total, 8), jnp.int32).astype(bf16)
    keep[2 * SLOTS :, :] = eighths
    send[2 * SLOTS :, :] = eighths


def join_body(pos, keep, recv, cot, gate_keep, gate_send, up_keep, up_send):
    cot[:SLOTS, :] = keep[:SLOTS, :]
    cot[SLOTS:, :] = recv[:SLOTS, :]
    x = jnp.concatenate([keep[SLOTS : 2 * SLOTS, :], recv[SLOTS : 2 * SLOTS, :]], axis=0).astype(f32)
    of_y = [columns(x, [z * NY + y for z in range(NZ)]) for y in range(NY)]
    n = (keep[2 * SLOTS :, :QUART].astype(f32) + recv[2 * SLOTS :, :QUART].astype(f32)).astype(bf16)

    def pick(y):
        low = jnp.where(y == 0, of_y[0], of_y[1])
        return jnp.where(y < 2, low, jnp.where(y == 2, of_y[2], of_y[3]))

    y = pos[1]
    even = lax.rem(y, 2) == 0
    mine, flip = pick(y), pick(jnp.where(even, y + 1, y - 1))
    back, both = pick(3 - y), pick(3 - jnp.where(even, y + 1, y - 1))
    for out, l, r in (
        (gate_keep, mine, back),
        (gate_send, flip, both),
        (up_keep, mine, flip),
        (up_send, back, both),
    ):
        out[: 2 * SLOTS, :] = jnp.concatenate([l, r], axis=1).astype(bf16)
    gate_keep[2 * SLOTS :, :] = n
    gate_send[2 * SLOTS :, :] = n


def tok_body(gate_keep, gate_recv, up_keep, up_recv, tok, eighths):
    h = 2 * SLOTS
    for i, piece in enumerate((gate_keep, gate_recv, up_keep, up_recv)):
        tok[i * h : (i + 1) * h, :] = piece[:h, :]
    eighths[...] = gate_keep[h:, :128].astype(f32) + gate_recv[h:, :128].astype(f32)


def sets_body(tok, far, gate, up):
    h = 4 * SLOTS
    for i, piece in enumerate((tok, far)):
        gate[i * h : (i + 1) * h, :] = piece[:h, :]
        up[i * h : (i + 1) * h, :] = piece[h:, :]


def put_count(send, at, n):
    high = jnp.floor(n * (1.0 / 32.0))
    send[at:, :] = jnp.zeros((16, FF), bf16)
    send[at:, :128] = high.astype(bf16)
    send[at:, 128:256] = (n - 32.0 * high).astype(bf16)


def get_count(recv, at):
    return 32.0 * recv[at:, :128].astype(f32) + recv[at:, 128:256].astype(f32)


T_SHIFTS = [(dw, dx) for dw in range(NW) for dx in range(NX)]


def tensor_slot(pos, dw, dx):
    return lax.rem(pos[3] + dw, NW) * NX + lax.rem(pos[4] - dx + NX, NX)


def rows_of(pieces, d, at, count):
    mine, left, right, top, bottom = pieces
    half = top.shape[0]
    if d == 2:
        return top[at : at + count, :] if at < half else bottom[at - half : at - half + count, :]
    return (mine, left, None, right)[d][at : at + count, :]


def hidden_body(pos, *refs):
    cots, weights = refs[:5], refs[5:10]
    own, other, a, b = refs[10:]
    for dx in range(NX):
        for dw in range(NW):
            at = pl.multiple_of(tensor_slot(pos, dw, dx) * SLOTS, 16)
            for i in range(2):
                a[pl.ds(at + i * ROWS, SLOTS), :] = rows_of(cots, dx, (dw * 2 + i) * SLOTS, SLOTS)
    for dy in range(NY):
        y = lax.rem(pos[1] - dy + NY, NY)
        for dz in range(NZ):
            z = lax.rem(pos[0] - dz + NZ, NZ)
            to = pl.multiple_of((z * NY + y) * BLK, 16)
            b[pl.ds(to, BLK), :] = rows_of(weights, dy, dz * BLK, BLK)
    for part, out in ((1, other), (0, own)):
        for n in range(0, FF, 384):
            out[:, n : n + 384] = jnp.dot(
                a[part * ROWS : (part + 1) * ROWS, :], b[:, n : n + 384], preferred_element_type=f32
            )


def delta_body(own, recv, gate_pre, up_pre, gate_delta, up_delta, both):
    def step(i, carry):
        at = pl.ds(pl.multiple_of(i * 48, 16), 48)
        h = own[at, :] + recv[at, :]
        g, u = gate_pre[at, :].astype(f32), up_pre[at, :].astype(f32)
        sg = 1.0 / (1.0 + jnp.exp(-g))
        hs = h * sg
        gate_delta[at, :] = (hs * u * (1.0 + g * (1.0 - sg))).astype(bf16)
        up_delta[at, :] = (hs * g).astype(bf16)
        both[at, :] = gate_delta[at, :]
        both[pl.ds(pl.multiple_of(ROWS + i * 48, 16), 48), :] = up_delta[at, :]
        return carry

    lax.fori_loop(0, ROWS // 48, step, 0)


def turn_body(pos, *refs):
    pieces, (xt, x) = refs[:5], refs[5:]
    for dx in range(NX):
        for dw in range(NW):
            at = tensor_slot(pos, dw, dx) * SLOTS
            for s in range(4):
                to = pl.multiple_of(at + s * ROWS, 16)
                x[pl.ds(to, SLOTS), :] = rows_of(pieces, dx, (dw * 4 + s) * SLOTS, SLOTS)
    for a in range(0, 4 * ROWS, 128):
        xt[:, a : a + 128] = x[a : a + 128, :].T


def grad_part(xt, deltas, keep, send):
    for part, out in ((1, send), (0, keep)):
        for n in range(0, FF, 384):
            acc = None
            for s, d in enumerate(deltas):
                term = jnp.dot(
                    xt[part * 320 : (part + 1) * 320, s * ROWS : (s + 1) * ROWS],
                    d[:, n : n + 384],
                    preferred_element_type=f32,
                )
                acc = term if acc is None else acc + term
            out[:320, n : n + 384] = acc.astype(out.dtype)


def gate_grad_body(xt, d0, d1, d2, d3, eighths, keep, send):
    grad_part(xt, (d0, d1.at[:ROWS], d2, d3), keep, send)
    put_count(send, 320, eighths[...])


def up_grad_body(xt, d0, d1, d2, d3, keep, send):
    grad_part(xt, (d0, d1.at[ROWS:], d2, d3), keep, send)


def ysum(pos, keep, recv, own, send):
    z = pos[0]
    z1 = jnp.where(lax.rem(z, 2) == 0, z + 1, z - 1)
    for out, first in ((send, z1), (own, z)):
        for half, block in ((0, first), (1, lax.rem(first + 2, NZ))):
            at = pl.ds(pl.multiple_of(block * BLK, 16), BLK)
            out[half * BLK : (half + 1) * BLK, :] = (keep[at, :] + recv[at, :].astype(f32)).astype(out.dtype)


def gate_ysum_body(pos, keep, recv, n, own, send, n_out):
    ysum(pos, keep, recv, own, send)
    n_out[...] = n[...] + get_count(recv, 320)
    put_count(send, 2 * BLK, n_out[...])


def up_ysum_body(pos, keep, recv, own, send):
    ysum(pos, keep, recv, own, send)


def zsum(keep, recv, own, send):
    send[:BLK, :] = (keep[BLK:, :] + recv[BLK : 2 * BLK, :].astype(f32)).astype(bf16)
    own[...] = keep[:BLK, :] + recv[:BLK, :].astype(f32)


def gate_zsum_body(keep, recv, n, own, send, n_out):
    zsum(keep, recv, own, send)
    n_out[...] = n[...] + get_count(recv, 2 * BLK)
    put_count(send, BLK, n_out[...])


def up_zsum_body(keep, recv, own, send):
    zsum(keep, recv, own, send)


def gate_final_body(own, recv, n, out, inverse):
    total = 8.0 * (n[...] + get_count(recv, BLK))
    inverse[...] = 1.0 / total
    out[...] = (own[...] + recv[:BLK, :].astype(f32)) * inverse[0:1, 0:1]


def up_final_body(own, recv, inverse, out):
    out[...] = (own[...] + recv[...].astype(f32)) * inverse[0:1, 0:1]


def x_move(x, d):
    return tp_move(x, lambda w, k: (w, (k + d) % NX))


def y_move(x, d):
    return dp_move(x, lambda z, y, c: (z, (y + d) % NY, c))


def ring(x, move):
    half = x.shape[0] // 2
    left, right = move(x, 1), move(x, -1)
    return x, left, right, move(left[:half], 1), move(right[half:], -1)


def w_move(x):
    return tp_move(x, lambda w, k: (1 - w, k))


def after(x, *others):
    return lax.optimization_barrier((x, *others))[0]


def local(tokens, cotangent, gate_pre, up_pre, down_weight, counts):
    dp, tp = lax.axis_index("dp"), lax.axis_index("tensor")
    pos = jnp.stack([dp // 8, dp // 2 % 4, dp % 2, tp // 4, tp % 4]).astype(jnp.int32)

    w_z = [dp_move(down_weight, lambda z, y, c: ((z + dz) % NZ, y, c)) for dz in (1, 2, 3)]
    both = sds((2 * SLOTS + 16, HALF), bf16)
    keep, send = call(split_body, (both, both), 2, 2)(pos, counts, cotangent, tokens)
    quart = sds((2 * SLOTS, QUART), bf16)
    quart_n = sds((2 * SLOTS + 16, QUART), bf16)
    cot, gate_keep, gate_send, up_keep, up_send = call(
        join_body, (sds((2 * SLOTS, HALF), bf16), quart_n, quart_n, quart, quart), 1, 2
    )(pos, keep, core_swap(send))
    far = w_move(cot)
    cots = ring(jnp.concatenate([cot, far], axis=0), x_move)
    gate_recv = dp_move(gate_send, GATE_PAIR)
    up_recv = dp_move(up_send, UP_PAIR)
    tok, eighths = call(tok_body, (sds((8 * SLOTS, QUART), bf16), sds((16, 128), f32)), 0, 4)(
        gate_keep, gate_recv, up_keep, up_recv
    )
    w_z, tok = lax.optimization_barrier((w_z, tok))
    weights = ring(jnp.concatenate([down_weight, *w_z], axis=0), y_move)
    tok_far = w_move(after(tok, far))
    tset = sds((8 * SLOTS, QUART), bf16)
    gate_set, up_set = call(sets_body, (tset, tset), 0, 2)(tok, tok_far)
    gate_toks = ring(after(gate_set, *cots), x_move)
    up_toks = ring(after(up_set, *gate_toks), x_move)

    weights = lax.optimization_barrier((*weights, gate_set))[:5]
    hid = sds((ROWS, FF), f32)
    own, other = call(
        hidden_body,
        (hid, hid),
        1,
        10,
        [pltpu.VMEM((2 * ROWS, HALF), bf16), pltpu.VMEM((HALF, FF), bf16)],
        flops=2 * 2 * ROWS * HALF * FF,
        nbytes=8 << 20,
    )(pos, *cots, *weights)
    recv = core_swap(other)
    delta = sds((ROWS, FF), bf16)
    gate_delta, up_delta, both = call(delta_body, (delta, delta, sds((2 * ROWS, FF), bf16)), 0, 4, nbytes=6 << 20)(
        own, recv, gate_pre, up_pre
    )

    xt = sds((QUART, 4 * ROWS), bf16)
    turn = call(turn_body, xt, 1, 5, [pltpu.VMEM((4 * ROWS, QUART), bf16)])
    cost = dict(flops=2 * 4 * ROWS * QUART * FF, nbytes=8 << 20)
    n = sds((16, 128), f32)

    e = dp_move(gate_delta, GATE_PAIR)
    f = dp_move(up_delta, UP_PAIR)
    other = core_swap(both)
    gate = (gate_delta, other, e, core_swap(e))
    up = (up_delta, other, f, core_swap(f))

    def z1(x):
        return dp_move(x, lambda z, y, c: (z ^ 1, y, c))

    def z2(x):
        return dp_move(x, lambda z, y, c: (z ^ 2, y, c))

    keep, send = call(gate_grad_body, (sds((320, FF), f32), sds((336, FF), bf16)), 0, 6, **cost)(
        turn(pos, *gate_toks), *gate, eighths
    )
    got = dp_move(send, UP_PAIR)
    keep, send, eighths = call(gate_ysum_body, (sds((2 * BLK, FF), f32), sds((2 * BLK + 16, FF), bf16), n), 1, 3)(
        pos, keep, got, eighths
    )
    got = z1(send)
    keep, send, eighths = call(gate_zsum_body, (sds((BLK, FF), f32), sds((BLK + 16, FF), bf16), n), 0, 3)(
        keep, got, eighths
    )
    grad_gate, inverse = call(gate_final_body, (sds((BLK, FF), f32), n), 0, 3)(keep, z2(send), eighths)

    keep, send = call(up_grad_body, (sds((320, FF), f32), sds((320, FF), bf16)), 0, 5, **cost)(
        turn(pos, *up_toks), *up
    )
    got = dp_move(send, GATE_PAIR)
    keep, send = call(up_ysum_body, (sds((2 * BLK, FF), f32), sds((2 * BLK, FF), bf16)), 1, 2)(pos, keep, got)
    got = z1(send)
    keep, send = call(up_zsum_body, (sds((BLK, FF), f32), sds((BLK, FF), bf16)), 0, 2)(keep, got)
    grad_up = call(up_final_body, sds((BLK, FF), f32), 0, 3)(keep, z2(send), inverse)
    return grad_gate, grad_up


def solution(mesh):
    rows = P(("dp", "tensor"), None)
    both = P("dp", "tensor")
    return jax.shard_map(
        local,
        mesh=mesh,
        in_specs=(rows, rows, both, both, both, P("dp", None)),
        out_specs=(both, both),
        check_vma=False,
    )
```

time: 580 us -> 176 us (0.30)
  waiting for transfers between devices: 433 us -> 85 us
  blocking collectives: 76.9 us -> 0 us
  starting transfers between devices: 0.19 us -> 62.2 us
  local copies, waits for them, and re-layouts: 28.7 us -> 3.86 us
  matrix products: 23.6 us -> 0 us
  Pallas kernels: 0 us -> 20.9 us
  between operations: 15.2 us -> 0.99 us
    unnamed x7 -> x0, waiting for transfers between devices: 303 us -> none
    all_gather x3 -> x0, waiting for transfers between devices: 130 us -> none  [the longest x1 68.8 us: local(): lax.all_gather(tokens, 'tensor', axis=0, tiled=True)]
    ppermute x0 -> x36, waiting for transfers between devices: none -> 85 us  [the longest x22 43.5 us: dp_move(): return lax.ppermute(x, 'dp', pairs)]
    psum x1 -> x0, blocking collectives: 76.9 us -> none  [local(): total = lax.psum(own_total, 'dp')]
    ppermute x0 -> x36, starting transfers between devices: none -> 62.2 us  [the longest x14 31.2 us: tp_move(): return lax.ppermute(x, 'tensor', pairs)]
    unnamed x8 -> x14, local copies, waits for them, and re-layouts: 28.6 us -> 3.55 us
    dot_general x3 -> x0, matrix products: 23.6 us -> none  [the longest x2 17.6 us: rows_product(): lax.dot_general(left, right, (((0,), (0,)), ((), ())), preferred_element_...]
    pallas_call x0 -> x16, Pallas kernels: none -> 20.9 us  [the longest x1 4.07 us: local(): call(hidden_body, (hid, hid), 1, 10, [pltpu.VMEM((2 * ROWS, HALF), bf16),...]
  transfers between devices with their start and end apart: 5 -> 36, of which waited for: 4 -> 16; matrix products, arithmetic and copies ran while one was open for 5% -> 1% of each run, Pallas kernels for 0% -> 8%
where the time goes in v1:
time: 176 us; the launch traced here: 173 us
  waiting for transfers between devices  85 us (48%)
  starting transfers between devices  62.2 us (35%)
  Pallas kernels  20.9 us (12%)
  local copies, waits for them, and re-layouts  3.86 us (2%)
    ppermute x22, waiting for transfers between devices, dp_move(): return lax.ppermute(x, 'dp', pairs)  43.5 us
    ppermute x14, waiting for transfers between devices, tp_move(): return lax.ppermute(x, 'tensor', pairs)  41.5 us
    ppermute x14, starting transfers between devices, tp_move(): return lax.ppermute(x, 'tensor', pairs)  31.2 us
    ppermute x22, starting transfers between devices, dp_move(): return lax.ppermute(x, 'dp', pairs)  31 us
    pallas_call x1, Pallas kernels, local(): call(hidden_body, (hid, hid), 1, 10, [pltpu.VMEM((2 * ROWS, HALF), bf16),...  4.07 us
    pallas_call x1, Pallas kernels, local(): call(gate_grad_body, (sds((320, FF), f32), sds((336, FF), bf16)), 0, 6, *...  3.82 us
    pallas_call x1, Pallas kernels, local(): call(up_grad_body, (sds((320, FF), f32), sds((320, FF), bf16)), 0, 5, **c...  3.79 us
    unnamed x14, local copies, waits for them, and re-layouts  3.55 us
  transfers between devices with their start and end apart: 36, of which 16 were waited for; matrix products, arithmetic and copies ran while one was open for 1% of the time, Pallas kernels for 8%

profile of v1, /device:TPU:4, one launch (start us, length us, event | category | flops | bytes accessed | tf_op | source)
XLA Modules:
  0.0 173.0 jit_solution(12198966918159270834)
XLA Ops:
  6.3 3.3 %collective-permute-start.1 = (bf16[80,1152]{1,0:T(8,128)(2,1)}, bf16[80,1152]{1,0:T(8,128)(2,1)S(1)}, u32[]{:S(2)}, u32[]{:S(2)}) collective-permute-start(bf16[80,1152]{1,0:T(8,128)(2,1)} %param.10), channel_id=1, source_target_pairs={{0,128},{8,136},{16,144},{24,152},{32,160},{40,168},{48,176},{56,1... | collective-permute-start | bytes 552968 | tf_op jit(solution)/shard_map/ppermute | solution.py:24
  16.3 3.0 %collective-permute-done.5.up_recv = bf16[96,640]{1,0:T(8,128)(2,1)S(1)} collective-permute-done((bf16[96,640]{1,0:T(8,128)(2,1)S(1)}, bf16[96,640]{1,0:T(8,128)(2,1)S(1)}, u32[]{:S(2)}, u32[]{:S(2)}) %collective-permute-start.5) | collective-permute-done | bytes 122912 | tf_op jit(solution)/shard_map/ppermute | solution.py:24
  19.2 5.4 %collective-permute-start.6 = (bf16[96,1280]{1,0:T(8,128)(2,1)S(1)}, bf16[96,1280]{1,0:T(8,128)(2,1)S(1)}, u32[]{:S(2)}, u32[]{:S(2)}) collective-permute-start(bf16[96,1280]{1,0:T(8,128)(2,1)S(1)} %get-tuple-element.54), channel_id=1, source_target_pairs={{0,4},{1,5},{2,6},{3,7},{4,0},{5,1},{6,2},{7,3},{8,12},{9,13},{10,... | collective-permute-start | bytes 737288 | tf_op jit(solution)/shard_map/ppermute | solution.py:33
  24.9 3.2 %collective-permute-start.17 = (bf16[320,1152]{1,0:T(8,128)(2,1)S(1)}, bf16[320,1152]{1,0:T(8,128)(2,1)S(1)}, u32[]{:S(2)}, u32[]{:S(2)}) collective-permute-start(bf16[320,1152]{1,0:T(8,128)(2,1)S(1)} %constant_dynamic-update-slice_fusion.2.refs_5_), channel_id=1, source_target_pairs={{0,48},{8,56},{16,0},{24,8},{32,16},{40,24},{48,32},{56,40},{64,11... | collective-permute-start | bytes 2211848 | tf_op jit(solution)/shard_map/ppermute | solution.py:24
  28.1 3.0 %collective-permute-done.6 = bf16[96,1280]{1,0:T(8,128)(2,1)S(1)} collective-permute-done((bf16[96,1280]{1,0:T(8,128)(2,1)S(1)}, bf16[96,1280]{1,0:T(8,128)(2,1)S(1)}, u32[]{:S(2)}, u32[]{:S(2)}) %collective-permute-start.6) | collective-permute-done | bytes 245792 | tf_op jit(solution)/shard_map/ppermute | solution.py:33
  33.3 11.3 %collective-permute-start.7 = (bf16[384,640]{1,0:T(8,128)(2,1)S(1)}, bf16[384,640]{1,0:T(8,128)(2,1)S(1)}, u32[]{:S(2)}, u32[]{:S(2)}) collective-permute-start(bf16[384,640]{1,0:T(8,128)(2,1)S(1)} %get-tuple-element.55.tok), channel_id=1, source_target_pairs={{0,4},{1,5},{2,6},{3,7},{4,0},{5,1},{6,2},{7,3},{8,12},{9,13},{10,... | collective-permute-start | bytes 1474568 | tf_op jit(solution)/shard_map/ppermute | solution.py:33
  45.2 2.8 %collective-permute-start.19 = (bf16[160,1152]{1,0:T(8,128)(2,1)S(1)}, bf16[160,1152]{1,0:T(8,128)(2,1)S(1)}, u32[]{:S(2)}, u32[]{:S(2)}) collective-permute-start(bf16[160,1152]{1,0:T(8,128)(2,1)S(1)} %slice.37), channel_id=1, source_target_pairs={{0,48},{8,56},{16,0},{24,8},{32,16},{40,24},{48,32},{56,40},{64,11... | collective-permute-start | bytes 1105928 | tf_op jit(solution)/shard_map/ppermute | solution.py:24
  50.4 11.0 %collective-permute-done.7.far = bf16[384,640]{1,0:T(8,128)(2,1)S(1)} collective-permute-done((bf16[384,640]{1,0:T(8,128)(2,1)S(1)}, bf16[384,640]{1,0:T(8,128)(2,1)S(1)}, u32[]{:S(2)}, u32[]{:S(2)}) %collective-permute-start.7) | collective-permute-done | bytes 491552 | tf_op jit(solution)/shard_map/ppermute | solution.py:33
  61.6 4.1 %shard_map.82 = (f32[384,1152]{1,0:T(8,128)S(1)}, f32[384,1152]{1,0:T(8,128)S(1)}) custom-call(s32[5]{0:T(128)S(1)} %stack.23.pos, bf16[192,1280]{1,0:T(8,128)(2,1)S(1)} %constant_dynamic-update-slice_fusion.refs_0_, bf16[192,1280]{1,0:T(8,128)(2,1)S(1)} %collective-permute-done.8.refs_1_, bf16[192,1280]{1,0:T(8,128)(2,1)S(1)} %collective-permute-done.9.refs_2_, ...), custom_call_target="tpu_custom_call" | custom-call | flops 2264924160 | bytes 8388608 | tf_op jit(solution)/shard_map/pallas_call | solution.py:330
  65.8 3.7 %collective-permute-done.20.recv = f32[384,1152]{1,0:T(8,128)S(1)} collective-permute-done((f32[384,1152]{1,0:T(8,128)S(1)}, f32[384,1152]{1,0:T(8,128)S(1)}, u32[]{:S(2)}, u32[]{:S(2)}) %collective-permute-start.20) | collective-permute-done | bytes 1769504 | tf_op jit(solution)/shard_map/ppermute | solution.py:24
  76.1 10.9 %collective-permute-done.12.refs_1_ = bf16[384,640]{1,0:T(8,128)(2,1)S(1)} collective-permute-done((bf16[384,640]{1,0:T(8,128)(2,1)S(1)}, bf16[384,640]{1,0:T(8,128)(2,1)S(1)}, u32[]{:S(2)}, u32[]{:S(2)}) %collective-permute-start.12) | collective-permute-done | bytes 491552 | tf_op jit(solution)/shard_map/ppermute | solution.py:33
  89.2 4.0 %collective-permute-done.22.d2 = bf16[384,1152]{1,0:T(8,128)(2,1)S(1)} collective-permute-done((bf16[384,1152]{1,0:T(8,128)(2,1)S(1)}, bf16[384,1152]{1,0:T(8,128)(2,1)S(1)}, u32[]{:S(2)}, u32[]{:S(2)}) %collective-permute-start.22) | collective-permute-done | bytes 884768 | tf_op jit(solution)/shard_map/ppermute | solution.py:24
  96.1 3.0 %collective-permute-start.27 = (bf16[384,640]{1,0:T(8,128)(2,1)S(1)}, bf16[384,640]{1,0:T(8,128)(2,1)S(1)}, u32[]{:S(2)}, u32[]{:S(2)}) collective-permute-start(bf16[384,640]{1,0:T(8,128)(2,1)S(1)} %get-tuple-element.81.refs_0_), channel_id=1, source_target_pairs={{0,1},{1,2},{2,3},{3,0},{4,5},{5,6},{6,7},{7,4},{8,9},{9,10},{10,1... | collective-permute-start | bytes 1474568 | tf_op jit(solution)/shard_map/ppermute | solution.py:33
  99.0 8.8 %collective-permute-done.27.refs_1_ = bf16[384,640]{1,0:T(8,128)(2,1)S(1)} collective-permute-done((bf16[384,640]{1,0:T(8,128)(2,1)S(1)}, bf16[384,640]{1,0:T(8,128)(2,1)S(1)}, u32[]{:S(2)}, u32[]{:S(2)}) %collective-permute-start.27) | collective-permute-done | bytes 491552 | tf_op jit(solution)/shard_map/ppermute | solution.py:33
  107.8 2.6 %collective-permute-start.29 = (bf16[192,640]{1,0:T(8,128)(2,1)S(1)}, bf16[192,640]{1,0:T(8,128)(2,1)S(1)}, u32[]{:S(2)}, u32[]{:S(2)}) collective-permute-start(bf16[192,640]{1,0:T(8,128)(2,1)S(1)} %slice.38), channel_id=1, source_target_pairs={{0,1},{1,2},{2,3},{3,0},{4,5},{5,6},{6,7},{7,4},{8,9},{9,10},{10,1... | collective-permute-start | bytes 737288 | tf_op jit(solution)/shard_map/ppermute | solution.py:33
  114.1 2.8 %collective-permute-done.30.refs_4_ = bf16[192,640]{1,0:T(8,128)(2,1)S(1)} collective-permute-done((bf16[192,640]{1,0:T(8,128)(2,1)S(1)}, bf16[192,640]{1,0:T(8,128)(2,1)S(1)}, u32[]{:S(2)}, u32[]{:S(2)}) %collective-permute-start.30) | collective-permute-done | bytes 245792 | tf_op jit(solution)/shard_map/ppermute | solution.py:33
  118.2 3.8 %shard_map.84 = (f32[320,1152]{1,0:T(8,128)S(1)}, bf16[336,1152]{1,0:T(8,128)(2,1)S(1)}) custom-call(bf16[640,1536]{1,0:T(8,128)(2,1)S(1)} %shard_map.81.xt, bf16[384,1152]{1,0:T(8,128)(2,1)S(1)} %get-tuple-element.68.d0, bf16[768,1152]{1,0:T(8,128)(2,1)S(1)} %collective-permute-done.21.d1, bf16[384,1152]{1,0:T(8,128)(2,1)S(1)} %collective-permute-done.22.d2, ...), custom_call_target="tpu_custom_call" | custom-call | flops 2264924160 | bytes 8388608 | tf_op jit(solution)/shard_map/pallas_call | solution.py:362
  123.2 3.8 %shard_map.89 = (f32[320,1152]{1,0:T(8,128)S(1)}, bf16[320,1152]{1,0:T(8,128)(2,1)S(1)}) custom-call(bf16[640,1536]{1,0:T(8,128)(2,1)S(1)} %shard_map.88.xt, bf16[384,1152]{1,0:T(8,128)(2,1)S(1)} %get-tuple-element.82.d0, bf16[768,1152]{1,0:T(8,128)(2,1)S(1)} %collective-permute-done.21.d1, bf16[384,1152]{1,0:T(8,128)(2,1)S(1)} %collective-permute-done.31.d2, ...), custom_call_target="tpu_custom_call" | custom-call | flops 2264924160 | bytes 8388608 | tf_op jit(solution)/shard_map/pallas_call | solution.py:375
  127.4 10.6 %collective-permute-done.24.recv = bf16[336,1152]{1,0:T(8,128)(2,1)S(1)} collective-permute-done((bf16[336,1152]{1,0:T(8,128)(2,1)S(1)}, bf16[336,1152]{1,0:T(8,128)(2,1)S(1)}, u32[]{:S(2)}, u32[]{:S(2)}) %collective-permute-start.24) | collective-permute-done | bytes 774176 | tf_op jit(solution)/shard_map/ppermute | solution.py:24
  138.7 7.5 %collective-permute-start.25 = (bf16[176,1152]{1,0:T(8,128)(2,1)S(1)}, bf16[176,1152]{1,0:T(8,128)(2,1)S(1)}, u32[]{:S(2)}, u32[]{:S(2)}) collective-permute-start(bf16[176,1152]{1,0:T(8,128)(2,1)S(1)} %get-tuple-element.74), channel_id=1, source_target_pairs={{0,64},{8,72},{16,80},{24,88},{32,96},{40,104},{48,112},{56,120},{... | collective-permute-start | bytes 1216520 | tf_op jit(solution)/shard_map/ppermute | solution.py:24
  148.8 7.7 %collective-permute-done.25.recv = bf16[176,1152]{1,0:T(8,128)(2,1)S(1)} collective-permute-done((bf16[176,1152]{1,0:T(8,128)(2,1)S(1)}, bf16[176,1152]{1,0:T(8,128)(2,1)S(1)}, u32[]{:S(2)}, u32[]{:S(2)}) %collective-permute-start.25) | collective-permute-done | bytes 405536 | tf_op jit(solution)/shard_map/ppermute | solution.py:24
  156.7 6.9 %collective-permute-done.34.recv = bf16[160,1152]{1,0:T(8,128)(2,1)S(1)} collective-permute-done((bf16[160,1152]{1,0:T(8,128)(2,1)S(1)}, bf16[160,1152]{1,0:T(8,128)(2,1)S(1)}, u32[]{:S(2)}, u32[]{:S(2)}) %collective-permute-start.34) | collective-permute-done | bytes 368672 | tf_op jit(solution)/shard_map/ppermute | solution.py:24
  163.8 2.5 %collective-permute-done.26.recv = bf16[96,1152]{1,0:T(8,128)(2,1)S(1)} collective-permute-done((bf16[96,1152]{1,0:T(8,128)(2,1)S(1)}, bf16[96,1152]{1,0:T(8,128)(2,1)S(1)}, u32[]{:S(2)}, u32[]{:S(2)}) %collective-permute-start.26) | collective-permute-done | bytes 221216 | tf_op jit(solution)/shard_map/ppermute | solution.py:24
  167.1 5.1 %collective-permute-done.35.recv = bf16[80,1152]{1,0:T(8,128)(2,1)S(1)} collective-permute-done((bf16[80,1152]{1,0:T(8,128)(2,1)S(1)}, bf16[80,1152]{1,0:T(8,128)(2,1)S(1)}, u32[]{:S(2)}, u32[]{:S(2)}) %collective-permute-start.35) | collective-permute-done | bytes 184352 | tf_op jit(solution)/shard_map/ppermute | solution.py:24
  (89 shorter events, 41.3 us)
Async XLA Ops:
  4.3 20.4 %collective-permute-start = (bf16[80,1152]{1,0:T(8,128)(2,1)}, bf16[80,1152]{1,0:T(8,128)(2,1)S(1)}, u32[]{:S(2)}, u32[]{:S(2)}) collective-permute-start(bf16[80,1152]{1,0:T(8,128)(2,1)} %param.10), channel_id=1, source_target_pairs={{0,64},{8,72},{16,80},{24,88},{32,96},{40,104},{48,112},{56,120},{... | collective-permute-start | bytes 552968 | tf_op jit(solution)/shard_map/ppermute | solution.py:24
  6.3 18.4 %collective-permute-start.1 = (bf16[80,1152]{1,0:T(8,128)(2,1)}, bf16[80,1152]{1,0:T(8,128)(2,1)S(1)}, u32[]{:S(2)}, u32[]{:S(2)}) collective-permute-start(bf16[80,1152]{1,0:T(8,128)(2,1)} %param.10), channel_id=1, source_target_pairs={{0,128},{8,136},{16,144},{24,152},{32,160},{40,168},{48,176},{56,1... | collective-permute-start | bytes 552968 | tf_op jit(solution)/shard_map/ppermute | solution.py:24
  9.5 15.2 %collective-permute-start.2 = (bf16[80,1152]{1,0:T(8,128)(2,1)}, bf16[80,1152]{1,0:T(8,128)(2,1)S(1)}, u32[]{:S(2)}, u32[]{:S(2)}) collective-permute-start(bf16[80,1152]{1,0:T(8,128)(2,1)} %param.10), channel_id=1, source_target_pairs={{0,192},{8,200},{16,208},{24,216},{32,224},{40,232},{48,240},{56,2... | collective-permute-start | bytes 552968 | tf_op jit(solution)/shard_map/ppermute | solution.py:24
  11.5 13.1 %collective-permute-start.4 = (bf16[112,640]{1,0:T(8,128)(2,1)S(1)}, bf16[112,640]{1,0:T(8,128)(2,1)S(1)}, u32[]{:S(2)}, u32[]{:S(2)}) collective-permute-start(bf16[112,640]{1,0:T(8,128)(2,1)S(1)} %get-tuple-element.49), channel_id=1, source_target_pairs={{0,16},{8,24},{16,0},{24,8},{32,48},{40,56},{48,32},{56,40},{64,80... | collective-permute-start | bytes 430088 | tf_op jit(solution)/shard_map/ppermute | solution.py:24
  24.8 19.8 %collective-permute-start.16 = (bf16[320,1152]{1,0:T(8,128)(2,1)S(1)}, bf16[320,1152]{1,0:T(8,128)(2,1)S(1)}, u32[]{:S(2)}, u32[]{:S(2)}) collective-permute-start(bf16[320,1152]{1,0:T(8,128)(2,1)S(1)} %constant_dynamic-update-slice_fusion.2.refs_5_), channel_id=1, source_target_pairs={{0,16},{8,24},{16,32},{24,40},{32,48},{40,56},{48,0},{56,8},{64,80... | collective-permute-start | bytes 2211848 | tf_op jit(solution)/shard_map/ppermute | solution.py:24
  24.9 20.3 %collective-permute-start.17 = (bf16[320,1152]{1,0:T(8,128)(2,1)S(1)}, bf16[320,1152]{1,0:T(8,128)(2,1)S(1)}, u32[]{:S(2)}, u32[]{:S(2)}) collective-permute-start(bf16[320,1152]{1,0:T(8,128)(2,1)S(1)} %constant_dynamic-update-slice_fusion.2.refs_5_), channel_id=1, source_target_pairs={{0,48},{8,56},{16,0},{24,8},{32,16},{40,24},{48,32},{56,40},{64,11... | collective-permute-start | bytes 2211848 | tf_op jit(solution)/shard_map/ppermute | solution.py:24
  31.2 16.9 %collective-permute-start.8 = (bf16[192,1280]{1,0:T(8,128)(2,1)S(1)}, bf16[192,1280]{1,0:T(8,128)(2,1)S(1)}, u32[]{:S(2)}, u32[]{:S(2)}) collective-permute-start(bf16[192,1280]{1,0:T(8,128)(2,1)S(1)} %constant_dynamic-update-slice_fusion.refs_0_), channel_id=1, source_target_pairs={{0,1},{1,2},{2,3},{3,0},{4,5},{5,6},{6,7},{7,4},{8,9},{9,10},{10,1... | collective-permute-start | bytes 1474568 | tf_op jit(solution)/shard_map/ppermute | solution.py:33
  32.4 16.9 %collective-permute-start.9 = (bf16[192,1280]{1,0:T(8,128)(2,1)S(1)}, bf16[192,1280]{1,0:T(8,128)(2,1)S(1)}, u32[]{:S(2)}, u32[]{:S(2)}) collective-permute-start(bf16[192,1280]{1,0:T(8,128)(2,1)S(1)} %constant_dynamic-update-slice_fusion.refs_0_), channel_id=1, source_target_pairs={{0,3},{1,0},{2,1},{3,2},{4,7},{5,4},{6,5},{7,6},{8,11},{9,8},{10,9... | collective-permute-start | bytes 1474568 | tf_op jit(solution)/shard_map/ppermute | solution.py:33
  33.3 28.2 %collective-permute-start.7 = (bf16[384,640]{1,0:T(8,128)(2,1)S(1)}, bf16[384,640]{1,0:T(8,128)(2,1)S(1)}, u32[]{:S(2)}, u32[]{:S(2)}) collective-permute-start(bf16[384,640]{1,0:T(8,128)(2,1)S(1)} %get-tuple-element.55.tok), channel_id=1, source_target_pairs={{0,4},{1,5},{2,6},{3,7},{4,0},{5,1},{6,2},{7,3},{8,12},{9,13},{10,... | collective-permute-start | bytes 1474568 | tf_op jit(solution)/shard_map/ppermute | solution.py:33
  44.6 17.0 %collective-permute-start.18 = (bf16[160,1152]{1,0:T(8,128)(2,1)S(1)}, bf16[160,1152]{1,0:T(8,128)(2,1)S(1)}, u32[]{:S(2)}, u32[]{:S(2)}) collective-permute-start(bf16[160,1152]{1,0:T(8,128)(2,1)S(1)} %slice.36), channel_id=1, source_target_pairs={{0,16},{8,24},{16,32},{24,40},{32,48},{40,56},{48,0},{56,8},{64,80... | collective-permute-start | bytes 1105928 | tf_op jit(solution)/shard_map/ppermute | solution.py:24
  45.2 16.4 %collective-permute-start.19 = (bf16[160,1152]{1,0:T(8,128)(2,1)S(1)}, bf16[160,1152]{1,0:T(8,128)(2,1)S(1)}, u32[]{:S(2)}, u32[]{:S(2)}) collective-permute-start(bf16[160,1152]{1,0:T(8,128)(2,1)S(1)} %slice.37), channel_id=1, source_target_pairs={{0,48},{8,56},{16,0},{24,8},{32,16},{40,24},{48,32},{56,40},{64,11... | collective-permute-start | bytes 1105928 | tf_op jit(solution)/shard_map/ppermute | solution.py:24
  48.1 13.6 %collective-permute-start.10 = (bf16[96,1280]{1,0:T(8,128)(2,1)S(1)}, bf16[96,1280]{1,0:T(8,128)(2,1)S(1)}, u32[]{:S(2)}, u32[]{:S(2)}) collective-permute-start(bf16[96,1280]{1,0:T(8,128)(2,1)S(1)} %slice.32), channel_id=1, source_target_pairs={{0,1},{1,2},{2,3},{3,0},{4,5},{5,6},{6,7},{7,4},{8,9},{9,10},{10,1... | collective-permute-start | bytes 737288 | tf_op jit(solution)/shard_map/ppermute | solution.py:33
  49.4 12.3 %collective-permute-start.11 = (bf16[96,1280]{1,0:T(8,128)(2,1)S(1)}, bf16[96,1280]{1,0:T(8,128)(2,1)S(1)}, u32[]{:S(2)}, u32[]{:S(2)}) collective-permute-start(bf16[96,1280]{1,0:T(8,128)(2,1)S(1)} %slice.33), channel_id=1, source_target_pairs={{0,3},{1,0},{2,1},{3,2},{4,7},{5,4},{6,5},{7,6},{8,11},{9,8},{10,9... | collective-permute-start | bytes 737288 | tf_op jit(solution)/shard_map/ppermute | solution.py:33
  71.1 47.1 %collective-permute-start.21 = (bf16[768,1152]{1,0:T(8,128)(2,1)S(1)}, bf16[768,1152]{1,0:T(8,128)(2,1)S(1)}, u32[]{:S(2)}, u32[]{:S(2)}) collective-permute-start(bf16[768,1152]{1,0:T(8,128)(2,1)S(1)} %get-tuple-element.69), channel_id=1, source_target_pairs={{0,8},{8,0},{16,24},{24,16},{32,40},{40,32},{48,56},{56,48},{64,72... | collective-permute-start | bytes 5308424 | tf_op jit(solution)/shard_map/ppermute | solution.py:24
  71.3 21.9 %collective-permute-start.22 = (bf16[384,1152]{1,0:T(8,128)(2,1)S(1)}, bf16[384,1152]{1,0:T(8,128)(2,1)S(1)}, u32[]{:S(2)}, u32[]{:S(2)}) collective-permute-start(bf16[384,1152]{1,0:T(8,128)(2,1)S(1)} %get-tuple-element.68.d0), channel_id=1, source_target_pairs={{0,16},{8,24},{16,0},{24,8},{32,48},{40,56},{48,32},{56,40},{64,80... | collective-permute-start | bytes 2654216 | tf_op jit(solution)/shard_map/ppermute | solution.py:24
  71.9 27.1 %collective-permute-start.31 = (bf16[384,1152]{1,0:T(8,128)(2,1)S(1)}, bf16[384,1152]{1,0:T(8,128)(2,1)S(1)}, u32[]{:S(2)}, u32[]{:S(2)}) collective-permute-start(bf16[384,1152]{1,0:T(8,128)(2,1)S(1)} %get-tuple-element.82.d0), channel_id=1, source_target_pairs={{0,48},{8,56},{16,32},{24,40},{32,16},{40,24},{48,0},{56,8},{64,11... | collective-permute-start | bytes 2654216 | tf_op jit(solution)/shard_map/ppermute | solution.py:24
  74.1 12.9 %collective-permute-start.12 = (bf16[384,640]{1,0:T(8,128)(2,1)S(1)}, bf16[384,640]{1,0:T(8,128)(2,1)S(1)}, u32[]{:S(2)}, u32[]{:S(2)}) collective-permute-start(bf16[384,640]{1,0:T(8,128)(2,1)S(1)} %get-tuple-element.57.refs_0_), channel_id=1, source_target_pairs={{0,1},{1,2},{2,3},{3,0},{4,5},{5,6},{6,7},{7,4},{8,9},{9,10},{10,1... | collective-permute-start | bytes 1474568 | tf_op jit(solution)/shard_map/ppermute | solution.py:33
  75.3 13.0 %collective-permute-start.13 = (bf16[384,640]{1,0:T(8,128)(2,1)S(1)}, bf16[384,640]{1,0:T(8,128)(2,1)S(1)}, u32[]{:S(2)}, u32[]{:S(2)}) collective-permute-start(bf16[384,640]{1,0:T(8,128)(2,1)S(1)} %get-tuple-element.57.refs_0_), channel_id=1, source_target_pairs={{0,3},{1,0},{2,1},{3,2},{4,7},{5,4},{6,5},{7,6},{8,11},{9,8},{10,9... | collective-permute-start | bytes 1474568 | tf_op jit(solution)/shard_map/ppermute | solution.py:33
  93.3 24.9 %collective-permute-start.23 = (bf16[384,1152]{1,0:T(8,128)(2,1)S(1)}, bf16[384,1152]{1,0:T(8,128)(2,1)S(1)}, u32[]{:S(2)}, u32[]{:S(2)}) collective-permute-start(bf16[384,1152]{1,0:T(8,128)(2,1)S(1)} %collective-permute-done.22.d2), channel_id=1, source_target_pairs={{0,8},{8,0},{16,24},{24,16},{32,40},{40,32},{48,56},{56,48},{64,72... | collective-permute-start | bytes 2654216 | tf_op jit(solution)/shard_map/ppermute | solution.py:24
  99.0 24.1 %collective-permute-start.32 = (bf16[384,1152]{1,0:T(8,128)(2,1)S(1)}, bf16[384,1152]{1,0:T(8,128)(2,1)S(1)}, u32[]{:S(2)}, u32[]{:S(2)}) collective-permute-start(bf16[384,1152]{1,0:T(8,128)(2,1)S(1)} %collective-permute-done.31.d2), channel_id=1, source_target_pairs={{0,8},{8,0},{16,24},{24,16},{32,40},{40,32},{48,56},{56,48},{64,72... | collective-permute-start | bytes 2654216 | tf_op jit(solution)/shard_map/ppermute | solution.py:24
  122.0 15.9 %collective-permute-start.24 = (bf16[336,1152]{1,0:T(8,128)(2,1)S(1)}, bf16[336,1152]{1,0:T(8,128)(2,1)S(1)}, u32[]{:S(2)}, u32[]{:S(2)}) collective-permute-start(bf16[336,1152]{1,0:T(8,128)(2,1)S(1)} %get-tuple-element.72), channel_id=1, source_target_pairs={{0,48},{8,56},{16,32},{24,40},{32,16},{40,24},{48,0},{56,8},{64,11... | collective-permute-start | bytes 2322440 | tf_op jit(solution)/shard_map/ppermute | solution.py:24
  127.0 19.2 %collective-permute-start.33 = (bf16[320,1152]{1,0:T(8,128)(2,1)S(1)}, bf16[320,1152]{1,0:T(8,128)(2,1)S(1)}, u32[]{:S(2)}, u32[]{:S(2)}) collective-permute-start(bf16[320,1152]{1,0:T(8,128)(2,1)S(1)} %get-tuple-element.84), channel_id=1, source_target_pairs={{0,16},{8,24},{16,0},{24,8},{32,48},{40,56},{48,32},{56,40},{64,80... | collective-permute-start | bytes 2211848 | tf_op jit(solution)/shard_map/ppermute | solution.py:24
  138.7 17.8 %collective-permute-start.25 = (bf16[176,1152]{1,0:T(8,128)(2,1)S(1)}, bf16[176,1152]{1,0:T(8,128)(2,1)S(1)}, u32[]{:S(2)}, u32[]{:S(2)}) collective-permute-start(bf16[176,1152]{1,0:T(8,128)(2,1)S(1)} %get-tuple-element.74), channel_id=1, source_target_pairs={{0,64},{8,72},{16,80},{24,88},{32,96},{40,104},{48,112},{56,120},{... | collective-permute-start | bytes 1216520 | tf_op jit(solution)/shard_map/ppermute | solution.py:24
  146.8 16.7 %collective-permute-start.34 = (bf16[160,1152]{1,0:T(8,128)(2,1)S(1)}, bf16[160,1152]{1,0:T(8,128)(2,1)S(1)}, u32[]{:S(2)}, u32[]{:S(2)}) collective-permute-start(bf16[160,1152]{1,0:T(8,128)(2,1)S(1)} %get-tuple-element.86), channel_id=1, source_target_pairs={{0,64},{8,72},{16,80},{24,88},{32,96},{40,104},{48,112},{56,120},{... | collective-permute-start | bytes 1105928 | tf_op jit(solution)/shard_map/ppermute | solution.py:24
  (17 other events, 115.1 us)

commit v2 on v1

v2 whole, which is shorter than its diff:
```python
import jax
import jax.numpy as jnp
from jax import lax
from jax.experimental import pallas as pl
from jax.experimental.pallas import tpu as pltpu
from jax.sharding import PartitionSpec as P

NZ, NY, NC, NW, NX = 4, 4, 2, 2, 4
SLOTS = 48
BLK = 80
D = BLK * NZ * NY * NC
HALF = D // 2
QUART = D // 4
FF = 1152
ROWS = SLOTS * NW * NX
bf16, f32 = jnp.bfloat16, jnp.float32
def dp_move(x, fn):
    pairs = []
    for z in range(NZ):
        for y in range(NY):
            for c in range(NC):
                tz, ty, tc = fn(z, y, c)
                pairs.append(((z * NY + y) * NC + c, (tz * NY + ty) * NC + tc))
    return lax.ppermute(x, "dp", pairs)


def tp_move(x, fn):
    pairs = []
    for w in range(NW):
        for k in range(NX):
            tw, tk = fn(w, k)
            pairs.append((w * NX + k, tw * NX + tk))
    return lax.ppermute(x, "tensor", pairs)


def GATE_PAIR(z, y, c):
    return z, y ^ 1, c


def UP_PAIR(z, y, c):
    return z, 3 - y, c


def core_swap(x):
    return dp_move(x, lambda z, y, c: (z, y, 1 - c))


def vmem():
    return pl.BlockSpec(memory_space=pltpu.VMEM)


def smem():
    return pl.BlockSpec(memory_space=pltpu.SMEM)


def call(body, out_shape, n_smem, n_vmem, scratch=(), flops=0, nbytes=0, mb=40):
    return pl.pallas_call(
        body,
        out_shape=out_shape,
        in_specs=[smem()] * n_smem + [vmem()] * n_vmem,
        out_specs=jax.tree.map(lambda _: vmem(), out_shape),
        scratch_shapes=list(scratch),
        compiler_params=pltpu.CompilerParams(vmem_limit_bytes=mb << 20),
        cost_estimate=pl.CostEstimate(flops=flops, bytes_accessed=nbytes, transcendentals=0),
    )


def sds(shape, dtype):
    return jax.ShapeDtypeStruct(shape, dtype)


def columns(x, chosen):
    return jnp.concatenate([x[:, i * BLK : (i + 1) * BLK] for i in chosen], axis=1)


def choose(i, options):
    low = jnp.where(i == 0, options[0], options[1])
    return jnp.where(i < 2, low, jnp.where(i == 2, options[2], options[3]))


def half_blocks(core):
    return [chip * NC + core for chip in range(NZ * NY)]


def split_body(pos, counts, cot, tok, keep, send):
    live = counts[0, pos[3] * NX + pos[4]]
    row = lax.broadcasted_iota(jnp.int32, (SLOTS, 1), 0)
    first = pos[2] == 0
    cot_rows = jnp.where(row < live, cot[...].astype(f32), 0.0)
    for at, x in ((0, cot_rows), (SLOTS, tok[...].astype(f32))):
        even, odd = columns(x, half_blocks(0)), columns(x, half_blocks(1))
        keep[at : at + SLOTS, :] = jnp.where(first, even, odd).astype(bf16)
        send[at : at + SLOTS, :] = jnp.where(first, odd, even).astype(bf16)
    total = counts[0, 0]
    for m in range(1, 8):
        total += counts[0, m]
    eighths = jnp.full((16, HALF), lax.div(total, 8), jnp.int32).astype(bf16)
    keep[2 * SLOTS :, :] = eighths
    send[2 * SLOTS :, :] = eighths


def join_body(pos, keep, recv, cot, gate_keep, gate_send, up_keep, up_send):
    cot[:SLOTS, :] = keep[:SLOTS, :]
    cot[SLOTS:, :] = recv[:SLOTS, :]
    x = jnp.concatenate([keep[SLOTS : 2 * SLOTS, :], recv[SLOTS : 2 * SLOTS, :]], axis=0).astype(f32)
    z_orders = [[z ^ k for k in (1, 3, 0, 2)] for z in range(NZ)]
    of_y = [
        choose(pos[0], [columns(x, [zz * NY + y for zz in order]) for order in z_orders]) for y in range(NY)
    ]
    n = (keep[2 * SLOTS :, :QUART].astype(f32) + recv[2 * SLOTS :, :QUART].astype(f32)).astype(bf16)

    y = pos[1]
    even = lax.rem(y, 2) == 0
    flipped = jnp.where(even, y + 1, y - 1)
    mine, flip, back, both = [choose(at, of_y) for at in (y, flipped, 3 - y, 3 - flipped)]
    for out, l, r in (
        (gate_keep, back, mine),
        (gate_send, both, flip),
        (up_keep, flip, mine),
        (up_send, both, back),
    ):
        out[: 2 * SLOTS, :] = jnp.concatenate([l, r], axis=1).astype(bf16)
    gate_keep[2 * SLOTS :, :] = n
    gate_send[2 * SLOTS :, :] = n


def tok_body(gate_keep, gate_recv, up_keep, up_recv, tok, eighths):
    h = 2 * SLOTS
    for i, piece in enumerate((gate_keep, gate_recv, up_keep, up_recv)):
        tok[i * h : (i + 1) * h, :] = piece[:h, :]
    eighths[...] = gate_keep[h:, :128].astype(f32) + gate_recv[h:, :128].astype(f32)


def slab_body(*refs):
    for i, piece in enumerate(refs[:4]):
        refs[4][i * BLK : (i + 1) * BLK, :] = piece[...]


def relay_body(left, far_left, right, far_right, gate, up):
    h = 4 * SLOTS
    gate[:h, :], gate[h:, :] = left[:h, :], far_left[:h, :]
    up[:h, :], up[h:, :] = right[h:, :], far_right[h:, :]


def put_count(send, at, n):
    high = jnp.floor(n * (1.0 / 32.0))
    send[at:, :] = jnp.zeros((16, FF), bf16)
    send[at:, :128] = high.astype(bf16)
    send[at:, 128:256] = (n - 32.0 * high).astype(bf16)


def get_count(recv, at):
    return 32.0 * recv[at:, :128].astype(f32) + recv[at:, 128:256].astype(f32)


T_SHIFTS = [(dw, dx) for dw in range(NW) for dx in range(NX)]


def tensor_slot(pos, dw, dx):
    return lax.rem(pos[3] + dw, NW) * NX + lax.rem(pos[4] - dx + NX, NX)


def rows_of(pieces, d, at, count):
    mine, left, right, top, bottom = pieces
    half = top.shape[0]
    if d == 2:
        return top[at : at + count, :] if at < half else bottom[at - half : at - half + count, :]
    return (mine, left, None, right)[d][at : at + count, :]


def hidden_body(pos, *refs):
    cots, weights = refs[:5], refs[5:10]
    other, own_rows, b, a = refs[10:]
    for dx in range(NX):
        for dw in range(NW):
            at = pl.multiple_of(tensor_slot(pos, dw, dx) * SLOTS, 16)
            for i, to in enumerate((own_rows, a)):
                to[pl.ds(at, SLOTS), :] = rows_of(cots, dx, (dw * 2 + i) * SLOTS, SLOTS)
    for dy in range(NY):
        y = lax.rem(pos[1] - dy + NY, NY)
        for dz in range(NZ):
            z = pos[0] ^ dz
            to = pl.multiple_of((z * NY + y) * BLK, 16)
            b[pl.ds(to, BLK), :] = rows_of(weights, dy, dz * BLK, BLK)
    product(a, b, other)


def product(a, b, out):
    for n in range(0, FF, 384):
        out[:, n : n + 384] = jnp.dot(a[...], b[:, n : n + 384], preferred_element_type=f32)


def own_body(a, b, out):
    product(a, b, out)


def delta_body(own, recv, gate_pre, up_pre, gate_delta, up_delta, both):
    def step(i, carry):
        at = pl.ds(pl.multiple_of(i * 48, 16), 48)
        h = own[at, :] + recv[at, :]
        g, u = gate_pre[at, :].astype(f32), up_pre[at, :].astype(f32)
        sg = 1.0 / (1.0 + jnp.exp(-g))
        hs = h * sg
        gate_delta[at, :] = (hs * u * (1.0 + g * (1.0 - sg))).astype(bf16)
        up_delta[at, :] = (hs * g).astype(bf16)
        both[at, :] = gate_delta[at, :]
        both[pl.ds(pl.multiple_of(ROWS + i * 48, 16), 48), :] = up_delta[at, :]
        return carry

    lax.fori_loop(0, ROWS // 48, step, 0)


def turn(first, pos, *refs):
    near, far, opposite, xt, x = refs[:3], refs[3:6], refs[6], refs[7], refs[8]
    h = 4 * SLOTS
    for dx in range(NX):
        for dw, pieces in enumerate((near, far)):
            at = tensor_slot(pos, dw, dx) * SLOTS
            piece, base = (opposite, dw * h) if dx == 2 else ((pieces[0], pieces[1], None, pieces[2])[dx], first)
            for s in range(4):
                i = base + s * SLOTS
                x[pl.ds(pl.multiple_of(at + s * ROWS, 16), SLOTS), :] = piece[i : i + SLOTS, :]
    for a in range(0, 4 * ROWS, 128):
        xt[:, a : a + 128] = x[a : a + 128, :].T


def gate_turn_body(pos, *refs):
    turn(0, pos, *refs)


def up_turn_body(pos, *refs):
    turn(4 * SLOTS, pos, *refs)


GROUP = 2 * BLK


def add_product(acc, xt, deltas, first, rows, out):
    for n in range(0, FF, 384):
        total = None if acc is None else acc[rows, n : n + 384]
        for s, d in enumerate(deltas):
            at = (first + s) * ROWS
            term = jnp.dot(xt[rows, at : at + ROWS], d[:, n : n + 384], preferred_element_type=f32)
            total = term if total is None else total + term
        out[: rows.stop - rows.start, n : n + 384] = total.astype(out.dtype)


def gate_near_body(xt, d, other, acc):
    add_product(None, xt, (d, other.at[:ROWS]), 0, slice(0, QUART), acc)


def up_near_body(xt, d, other, acc):
    add_product(None, xt, (d, other.at[ROWS:]), 0, slice(0, QUART), acc)


def far_body(acc, xt, e, e2, send, keep):
    add_product(acc, xt, (e, e2), 2, slice(0, 2 * GROUP), send)
    add_product(acc, xt, (e, e2), 2, slice(2 * GROUP, 4 * GROUP), keep)


def gate_far_body(acc, xt, e, e2, eighths, send, keep):
    far_body(acc, xt, e, e2, send, keep)
    put_count(send, 2 * GROUP, eighths[...])


def z1(keep, recv, send, rest):
    send[:GROUP, :] = (keep[:GROUP, :] + recv[:GROUP, :].astype(f32)).astype(bf16)
    rest[...] = keep[GROUP:, :] + recv[GROUP : 2 * GROUP, :].astype(f32)


def gate_z1_body(keep, recv, n, send, rest, n_out):
    z1(keep, recv, send, rest)
    n_out[...] = n[...] + get_count(recv, 2 * GROUP)
    put_count(send, GROUP, n_out[...])


def up_z1_body(keep, recv, send, rest):
    z1(keep, recv, send, rest)


def z2(part, got, own, send):
    send[:BLK, :] = (part[BLK:, :] + got[BLK : 2 * BLK, :].astype(f32)).astype(bf16)
    own[...] = part[:BLK, :] + got[:BLK, :].astype(f32)


def gate_z2_body(part, got, n, own, send, n_out):
    z2(part, got, own, send)
    n_out[...] = n[...] + get_count(got, GROUP)
    put_count(send, BLK, n_out[...])


def up_z2_body(part, got, own, send):
    z2(part, got, own, send)


def gate_final_body(own, recv, n, out, inverse):
    total = 8.0 * (n[...] + get_count(recv, BLK))
    inverse[...] = 1.0 / total
    out[...] = (own[...] + recv[:BLK, :].astype(f32)) * inverse[0:1, 0:1]


def up_final_body(own, recv, inverse, out):
    out[...] = (own[...] + recv[...].astype(f32)) * inverse[0:1, 0:1]


def x_move(x, d):
    return tp_move(x, lambda w, k: (w, (k + d) % NX))


def y_move(x, d):
    return dp_move(x, lambda z, y, c: (z, (y + d) % NY, c))


def z_move(x, k):
    return dp_move(x, lambda z, y, c: (z ^ k, y, c))


def ring(x, move):
    half = x.shape[0] // 2
    left, right = move(x, 1), move(x, -1)
    return x, left, right, move(left[:half], 1), move(right[half:], -1)


def w_move(x):
    return tp_move(x, lambda w, k: (1 - w, k))


def after(x, *others):
    return lax.optimization_barrier((x, *others))[0]


def local(tokens, cotangent, gate_pre, up_pre, down_weight, counts):
    dp, tp = lax.axis_index("dp"), lax.axis_index("tensor")
    pos = jnp.stack([dp // 8, dp // 2 % 4, dp % 2, tp // 4, tp % 4]).astype(jnp.int32)

    w_z = [z_move(down_weight, k) for k in (1, 2, 3)]
    both = sds((2 * SLOTS + 16, HALF), bf16)
    keep, send = call(split_body, (both, both), 2, 2)(pos, counts, cotangent, tokens)
    quart = sds((2 * SLOTS, QUART), bf16)
    quart_n = sds((2 * SLOTS + 16, QUART), bf16)
    cot, gate_keep, gate_send, up_keep, up_send = call(
        join_body, (sds((2 * SLOTS, HALF), bf16), quart_n, quart_n, quart, quart), 1, 2
    )(pos, keep, core_swap(send))
    far = w_move(cot)
    gate_recv = dp_move(gate_send, GATE_PAIR)
    up_recv = dp_move(up_send, UP_PAIR)
    tok, eighths = call(tok_body, (sds((8 * SLOTS, QUART), bf16), sds((16, 128), f32)), 0, 4)(
        gate_keep, gate_recv, up_keep, up_recv
    )
    near = [tok, x_move(tok, 1), x_move(tok, -1)]
    slab = call(slab_body, sds((NZ * BLK, FF), bf16), 0, 4, flops=20_000_000_000)
    weights = ring(slab(down_weight, *w_z), y_move)
    cots = ring(after(jnp.concatenate([cot, far], axis=0), *near), x_move)
    tok_far = w_move(after(tok, far))
    tok_far_x = after(tok_far, *cots)
    away = [tok_far, x_move(tok_far_x, 1), x_move(tok_far_x, -1)]
    relay = sds((8 * SLOTS, QUART), bf16)
    gate_opposite, up_opposite = call(relay_body, (relay, relay), 0, 4, flops=20_000_000_000)(
        near[1], away[1], near[2], away[2]
    )
    gate_opposite, up_opposite = x_move(gate_opposite, 1), x_move(up_opposite, -1)

    weights = lax.optimization_barrier((*weights, tok_far))[:5]
    hid = sds((ROWS, FF), f32)
    other, own_rows, whole_weight = call(
        hidden_body,
        (hid, sds((ROWS, HALF), bf16), sds((HALF, FF), bf16)),
        1,
        10,
        [pltpu.VMEM((ROWS, HALF), bf16)],
        flops=2 * ROWS * HALF * FF,
        nbytes=8 << 20,
    )(pos, *cots, *weights)
    recv = core_swap(other)
    own = call(own_body, hid, 0, 2, flops=2 * ROWS * HALF * FF, nbytes=8 << 20)(own_rows, whole_weight)
    delta = sds((ROWS, FF), bf16)
    gate_delta, up_delta, both = call(delta_body, (delta, delta, sds((2 * ROWS, FF), bf16)), 0, 4, nbytes=6 << 20)(
        own, recv, gate_pre, up_pre
    )

    other = core_swap(both)
    e = dp_move(gate_delta, GATE_PAIR)
    f = dp_move(up_delta, UP_PAIR)

    xt = sds((QUART, 4 * ROWS), bf16)
    scratch = [pltpu.VMEM((4 * ROWS, QUART), bf16)]
    acc = sds((QUART, FF), f32)
    half = dict(flops=4 * ROWS * QUART * FF, nbytes=6 << 20)
    n = sds((16, 128), f32)
    part, part_n = sds((GROUP, FF), bf16), sds((GROUP + 16, FF), bf16)

    gate_xt = call(gate_turn_body, xt, 1, 7, scratch)(pos, *near, *away, gate_opposite)
    up_xt = call(up_turn_body, xt, 1, 7, scratch)(pos, *near, *away, up_opposite)
    gate_acc = call(gate_near_body, acc, 0, 3, **half)(gate_xt, gate_delta, other)
    up_acc = call(up_near_body, acc, 0, 3, **half)(up_xt, up_delta, other)
    e2, f2 = core_swap(after(e, gate_acc, up_acc)), core_swap(after(f, gate_acc, up_acc))

    kept, last = sds((2 * GROUP, FF), f32), sds((GROUP, FF), f32)
    send, gate_keep = call(gate_far_body, (sds((2 * GROUP + 16, FF), bf16), kept), 0, 5, **half)(
        gate_acc, gate_xt, e, e2, eighths
    )
    gate_got = dp_move(send, UP_PAIR)
    send, up_keep = call(far_body, (sds((2 * GROUP, FF), bf16), kept), 0, 4, **half)(up_acc, up_xt, f, f2)
    up_got = dp_move(send, GATE_PAIR)

    send, gate_keep, eighths = call(gate_z1_body, (part_n, last, n), 0, 3)(gate_keep, gate_got, eighths)
    gate_got = z_move(send, 1)
    send, up_keep = call(up_z1_body, (part, last), 0, 2)(up_keep, after(up_got, send))
    up_got = z_move(send, 1)

    mine = sds((BLK, FF), f32)
    own, send, eighths = call(gate_z2_body, (mine, sds((BLK + 16, FF), bf16), n), 0, 3)(gate_keep, gate_got, eighths)
    grad_gate, inverse = call(gate_final_body, (mine, n), 0, 3)(own, z_move(send, 2), eighths)
    own, send = call(up_z2_body, (mine, sds((BLK, FF), bf16)), 0, 2)(up_keep, up_got)
    grad_up = call(up_final_body, mine, 0, 3)(own, z_move(send, 2), inverse)
    return grad_gate, grad_up


def solution(mesh):
    rows = P(("dp", "tensor"), None)
    both = P("dp", "tensor")
    return jax.shard_map(
        local,
        mesh=mesh,
        in_specs=(rows, rows, both, both, both, P("dp", None)),
        out_specs=(both, both),
        check_vma=False,
    )
```

time: 176 us -> 169 us (0.960)
  the two profiles are of different devices: /device:TPU:4 before, /device:TPU:1 now
where the time goes in v2:
time: 169 us
  waiting for transfers between devices  84.2 us (50%)
  starting transfers between devices  59.8 us (35%)
  Pallas kernels  20.7 us (12%)
  local copies, waits for them, and re-layouts  3.65 us (2%)
    ppermute x22, waiting for transfers between devices, dp_move(): return lax.ppermute(x, 'dp', pairs)  54.1 us
    ppermute x22, starting transfers between devices, dp_move(): return lax.ppermute(x, 'dp', pairs)  36.4 us
    ppermute x12, waiting for transfers between devices, tp_move(): return lax.ppermute(x, 'tensor', pairs)  30.1 us
    ppermute x12, starting transfers between devices, tp_move(): return lax.ppermute(x, 'tensor', pairs)  23.4 us
    unnamed x12, local copies, waits for them, and re-layouts  3.47 us
  transfers between devices with their start and end apart: 34, of which 17 were waited for; matrix products, arithmetic and copies ran while one was open for 0% of the time, Pallas kernels for 10%

profile of v2, /device:TPU:1, one launch (start us, length us, event | category | flops | bytes accessed | tf_op | source)
XLA Modules:
  0.0 169.3 jit_solution(8035878182823429473)
XLA Ops:
  4.2 3.3 %collective-permute-start = (bf16[112,1280]{1,0:T(8,128)(2,1)S(1)}, bf16[112,1280]{1,0:T(8,128)(2,1)S(1)}, u32[]{:S(2)}, u32[]{:S(2)}) collective-permute-start(bf16[112,1280]{1,0:T(8,128)(2,1)S(1)} %get-tuple-element.47), channel_id=1, source_target_pairs={{0,8},{8,0},{16,24},{24,16},{32,40},{40,32},{48,56},{56,48},{64,72... | collective-permute-start | bytes 860168 | tf_op jit(solution)/shard_map/ppermute | solution.py:24
  14.9 3.2 %collective-permute-done.2.up_recv = bf16[96,640]{1,0:T(8,128)(2,1)S(1)} collective-permute-done((bf16[96,640]{1,0:T(8,128)(2,1)S(1)}, bf16[96,640]{1,0:T(8,128)(2,1)S(1)}, u32[]{:S(2)}, u32[]{:S(2)}) %collective-permute-start.2) | collective-permute-done | bytes 122912 | tf_op jit(solution)/shard_map/ppermute | solution.py:24
  18.0 5.8 %collective-permute-start.5 = (bf16[96,1280]{1,0:T(8,128)(2,1)S(1)}, bf16[96,1280]{1,0:T(8,128)(2,1)S(1)}, u32[]{:S(2)}, u32[]{:S(2)}) collective-permute-start(bf16[96,1280]{1,0:T(8,128)(2,1)S(1)} %get-tuple-element.53), channel_id=1, source_target_pairs={{0,4},{1,5},{2,6},{3,7},{4,0},{5,1},{6,2},{7,3},{8,12},{9,13},{10,... | collective-permute-start | bytes 737288 | tf_op jit(solution)/shard_map/ppermute | solution.py:33
  23.9 2.6 %collective-permute-start.4 = (bf16[384,640]{1,0:T(8,128)(2,1)S(1)}, bf16[384,640]{1,0:T(8,128)(2,1)S(1)}, u32[]{:S(2)}, u32[]{:S(2)}) collective-permute-start(bf16[384,640]{1,0:T(8,128)(2,1)S(1)} %get-tuple-element.54.refs_0_), channel_id=1, source_target_pairs={{0,3},{1,0},{2,1},{3,2},{4,7},{5,4},{6,5},{7,6},{8,11},{9,8},{10,9... | collective-permute-start | bytes 1474568 | tf_op jit(solution)/shard_map/ppermute | solution.py:33
  29.5 6.8 %collective-permute-done.5 = bf16[96,1280]{1,0:T(8,128)(2,1)S(1)} collective-permute-done((bf16[96,1280]{1,0:T(8,128)(2,1)S(1)}, bf16[96,1280]{1,0:T(8,128)(2,1)S(1)}, u32[]{:S(2)}, u32[]{:S(2)}) %collective-permute-start.5) | collective-permute-done | bytes 245792 | tf_op jit(solution)/shard_map/ppermute | solution.py:33
  39.4 3.4 %collective-permute-done.18.refs_7_ = bf16[320,1152]{1,0:T(8,128)(2,1)S(1)} collective-permute-done((bf16[320,1152]{1,0:T(8,128)(2,1)S(1)}, bf16[320,1152]{1,0:T(8,128)(2,1)S(1)}, u32[]{:S(2)}, u32[]{:S(2)}) %collective-permute-start.18) | collective-permute-done | bytes 737312 | tf_op jit(solution)/shard_map/ppermute | solution.py:24
  42.8 3.2 %collective-permute-start.20 = (bf16[160,1152]{1,0:T(8,128)(2,1)S(1)}, bf16[160,1152]{1,0:T(8,128)(2,1)S(1)}, u32[]{:S(2)}, u32[]{:S(2)}) collective-permute-start(bf16[160,1152]{1,0:T(8,128)(2,1)S(1)} %slice.19), channel_id=1, source_target_pairs={{0,48},{8,56},{16,0},{24,8},{32,16},{40,24},{48,32},{56,40},{64,11... | collective-permute-start | bytes 1105928 | tf_op jit(solution)/shard_map/ppermute | solution.py:24
  47.0 3.7 %collective-permute-start.10 = (bf16[96,1280]{1,0:T(8,128)(2,1)S(1)}, bf16[96,1280]{1,0:T(8,128)(2,1)S(1)}, u32[]{:S(2)}, u32[]{:S(2)}) collective-permute-start(bf16[96,1280]{1,0:T(8,128)(2,1)S(1)} %slice.17), channel_id=1, source_target_pairs={{0,3},{1,0},{2,1},{3,2},{4,7},{5,4},{6,5},{7,6},{8,11},{9,8},{10,9... | collective-permute-start | bytes 737288 | tf_op jit(solution)/shard_map/ppermute | solution.py:33
  51.5 2.5 %collective-permute-done.19.refs_8_ = bf16[160,1152]{1,0:T(8,128)(2,1)S(1)} collective-permute-done((bf16[160,1152]{1,0:T(8,128)(2,1)S(1)}, bf16[160,1152]{1,0:T(8,128)(2,1)S(1)}, u32[]{:S(2)}, u32[]{:S(2)}) %collective-permute-start.19) | collective-permute-done | bytes 368672 | tf_op jit(solution)/shard_map/ppermute | solution.py:24
  54.0 3.3 %collective-permute-done.9.refs_3_ = bf16[96,1280]{1,0:T(8,128)(2,1)S(1)} collective-permute-done((bf16[96,1280]{1,0:T(8,128)(2,1)S(1)}, bf16[96,1280]{1,0:T(8,128)(2,1)S(1)}, u32[]{:S(2)}, u32[]{:S(2)}) %collective-permute-start.9) | collective-permute-done | bytes 245792 | tf_op jit(solution)/shard_map/ppermute | solution.py:33
  57.3 2.6 %shard_map.83 = (f32[384,1152]{1,0:T(8,128)S(1)}, bf16[384,1280]{1,0:T(8,128)(2,1)S(1)}, bf16[1280,1152]{1,0:T(8,128)(2,1)S(1)}) custom-call(s32[5]{0:T(128)S(1)} %stack.23.pos, bf16[192,1280]{1,0:T(8,128)(2,1)S(1)} %pad_maximum_fusion.refs_0_, bf16[192,1280]{1,0:T(8,128)(2,1)S(1)} %collective-permute-done.7.refs_1_, ...), custom_call_target="tpu_custom_call" | custom-call | flops 1132462080 | bytes 8388608 | tf_op jit(solution)/shard_map/pallas_call | solution.py:365
  59.9 4.6 %collective-permute-start.21 = (f32[384,1152]{1,0:T(8,128)S(1)}, f32[384,1152]{1,0:T(8,128)S(1)}, u32[]{:S(2)}, u32[]{:S(2)}) collective-permute-start(f32[384,1152]{1,0:T(8,128)S(1)} %get-tuple-element.65), channel_id=1, source_target_pairs={{0,8},{8,0},{16,24},{24,16},{32,40},{40,32},{48,56},{56,48},{64,72... | collective-permute-start | bytes 5308424 | tf_op jit(solution)/shard_map/ppermute | solution.py:24
  64.5 7.9 %collective-permute-start.12 = (bf16[384,640]{1,0:T(8,128)(2,1)S(1)}, bf16[384,640]{1,0:T(8,128)(2,1)S(1)}, u32[]{:S(2)}, u32[]{:S(2)}) collective-permute-start(bf16[384,640]{1,0:T(8,128)(2,1)S(1)} %collective-permute-done.6.refs_3_), channel_id=1, source_target_pairs={{0,3},{1,0},{2,1},{3,2},{4,7},{5,4},{6,5},{7,6},{8,11},{9,8},{10,9... | collective-permute-start | bytes 1474568 | tf_op jit(solution)/shard_map/ppermute | solution.py:33
  76.0 2.7 %collective-permute-start.29 = (bf16[384,1152]{1,0:T(8,128)(2,1)S(1)}, bf16[384,1152]{1,0:T(8,128)(2,1)S(1)}, u32[]{:S(2)}, u32[]{:S(2)}) collective-permute-start(bf16[384,1152]{1,0:T(8,128)(2,1)S(1)} %get-tuple-element.69.d), channel_id=1, source_target_pairs={{0,48},{8,56},{16,32},{24,40},{32,16},{40,24},{48,0},{56,8},{64,11... | collective-permute-start | bytes 2654216 | tf_op jit(solution)/shard_map/ppermute | solution.py:24
  79.3 3.7 %collective-permute-done.12.far_right.refs_5_ = bf16[384,640]{1,0:T(8,128)(2,1)S(1)} collective-permute-done((bf16[384,640]{1,0:T(8,128)(2,1)S(1)}, bf16[384,640]{1,0:T(8,128)(2,1)S(1)}, u32[]{:S(2)}, u32[]{:S(2)}) %collective-permute-start.12) | collective-permute-done | bytes 491552 | tf_op jit(solution)/shard_map/ppermute | solution.py:33
  83.0 3.1 %collective-permute-done.11.far_left.refs_4_ = bf16[384,640]{1,0:T(8,128)(2,1)S(1)} collective-permute-done((bf16[384,640]{1,0:T(8,128)(2,1)S(1)}, bf16[384,640]{1,0:T(8,128)(2,1)S(1)}, u32[]{:S(2)}, u32[]{:S(2)}) %collective-permute-start.11) | collective-permute-done | bytes 491552 | tf_op jit(solution)/shard_map/ppermute | solution.py:33
  87.7 10.1 %collective-permute-done.24.refs_6_ = bf16[384,640]{1,0:T(8,128)(2,1)S(1)} collective-permute-done((bf16[384,640]{1,0:T(8,128)(2,1)S(1)}, bf16[384,640]{1,0:T(8,128)(2,1)S(1)}, u32[]{:S(2)}, u32[]{:S(2)}) %collective-permute-start.24) | collective-permute-done | bytes 491552 | tf_op jit(solution)/shard_map/ppermute | solution.py:33
  110.8 2.8 %collective-permute-start.26 = (bf16[336,1152]{1,0:T(8,128)(2,1)S(1)}, bf16[336,1152]{1,0:T(8,128)(2,1)S(1)}, u32[]{:S(2)}, u32[]{:S(2)}) collective-permute-start(bf16[336,1152]{1,0:T(8,128)(2,1)S(1)} %get-tuple-element.73), channel_id=1, source_target_pairs={{0,48},{8,56},{16,32},{24,40},{32,16},{40,24},{48,0},{56,8},{64,11... | collective-permute-start | bytes 2322440 | tf_op jit(solution)/shard_map/ppermute | solution.py:24
  115.8 15.0 %collective-permute-done.26.recv = bf16[336,1152]{1,0:T(8,128)(2,1)S(1)} collective-permute-done((bf16[336,1152]{1,0:T(8,128)(2,1)S(1)}, bf16[336,1152]{1,0:T(8,128)(2,1)S(1)}, u32[]{:S(2)}, u32[]{:S(2)}) %collective-permute-start.26) | collective-permute-done | bytes 774176 | tf_op jit(solution)/shard_map/ppermute | solution.py:24
  131.0 4.1 %collective-permute-start.27 = (bf16[176,1152]{1,0:T(8,128)(2,1)S(1)}, bf16[176,1152]{1,0:T(8,128)(2,1)S(1)}, u32[]{:S(2)}, u32[]{:S(2)}) collective-permute-start(bf16[176,1152]{1,0:T(8,128)(2,1)S(1)} %get-tuple-element.75), channel_id=1, source_target_pairs={{0,64},{8,72},{16,80},{24,88},{32,96},{40,104},{48,112},{56,120},{... | collective-permute-start | bytes 1216520 | tf_op jit(solution)/shard_map/ppermute | solution.py:24
  135.4 8.2 %collective-permute-done.27.got = bf16[176,1152]{1,0:T(8,128)(2,1)S(1)} collective-permute-done((bf16[176,1152]{1,0:T(8,128)(2,1)S(1)}, bf16[176,1152]{1,0:T(8,128)(2,1)S(1)}, u32[]{:S(2)}, u32[]{:S(2)}) %collective-permute-start.27) | collective-permute-done | bytes 405536 | tf_op jit(solution)/shard_map/ppermute | solution.py:24
  143.7 3.1 %collective-permute-start.28 = (bf16[96,1152]{1,0:T(8,128)(2,1)S(1)}, bf16[96,1152]{1,0:T(8,128)(2,1)S(1)}, u32[]{:S(2)}, u32[]{:S(2)}) collective-permute-start(bf16[96,1152]{1,0:T(8,128)(2,1)S(1)} %get-tuple-element.78), channel_id=1, source_target_pairs={{0,128},{8,136},{16,144},{24,152},{32,160},{40,168},{48,176},{56,1... | collective-permute-start | bytes 663560 | tf_op jit(solution)/shard_map/ppermute | solution.py:24
  146.8 9.5 %collective-permute-done.32.got = bf16[160,1152]{1,0:T(8,128)(2,1)S(1)} collective-permute-done((bf16[160,1152]{1,0:T(8,128)(2,1)S(1)}, bf16[160,1152]{1,0:T(8,128)(2,1)S(1)}, u32[]{:S(2)}, u32[]{:S(2)}) %collective-permute-start.32) | collective-permute-done | bytes 368672 | tf_op jit(solution)/shard_map/ppermute | solution.py:24
  158.1 10.4 %collective-permute-done.33.recv = bf16[80,1152]{1,0:T(8,128)(2,1)S(1)} collective-permute-done((bf16[80,1152]{1,0:T(8,128)(2,1)S(1)}, bf16[80,1152]{1,0:T(8,128)(2,1)S(1)}, u32[]{:S(2)}, u32[]{:S(2)}) %collective-permute-start.33) | collective-permute-done | bytes 184352 | tf_op jit(solution)/shard_map/ppermute | solution.py:24
  (82 shorter events, 42.9 us)
Async XLA Ops:
  7.5 19.0 %collective-permute-start.15 = (bf16[80,1152]{1,0:T(8,128)(2,1)}, bf16[80,1152]{1,0:T(8,128)(2,1)S(1)}, u32[]{:S(2)}, u32[]{:S(2)}) collective-permute-start(bf16[80,1152]{1,0:T(8,128)(2,1)} %refs_0_.1), channel_id=1, source_target_pairs={{0,128},{8,136},{16,144},{24,152},{32,160},{40,168},{48,176},{56,1... | collective-permute-start | bytes 552968 | tf_op jit(solution)/shard_map/ppermute | solution.py:24
  8.8 17.7 %collective-permute-start.14 = (bf16[80,1152]{1,0:T(8,128)(2,1)}, bf16[80,1152]{1,0:T(8,128)(2,1)S(1)}, u32[]{:S(2)}, u32[]{:S(2)}) collective-permute-start(bf16[80,1152]{1,0:T(8,128)(2,1)} %refs_0_.1), channel_id=1, source_target_pairs={{0,64},{8,72},{16,80},{24,88},{32,96},{40,104},{48,112},{56,120},{... | collective-permute-start | bytes 552968 | tf_op jit(solution)/shard_map/ppermute | solution.py:24
  10.4 16.1 %collective-permute-start.16 = (bf16[80,1152]{1,0:T(8,128)(2,1)}, bf16[80,1152]{1,0:T(8,128)(2,1)S(1)}, u32[]{:S(2)}, u32[]{:S(2)}) collective-permute-start(bf16[80,1152]{1,0:T(8,128)(2,1)} %refs_0_.1), channel_id=1, source_target_pairs={{0,192},{8,200},{16,208},{24,216},{32,224},{40,232},{48,240},{56,2... | collective-permute-start | bytes 552968 | tf_op jit(solution)/shard_map/ppermute | solution.py:24
  12.2 11.6 %collective-permute-start.1 = (bf16[112,640]{1,0:T(8,128)(2,1)S(1)}, bf16[112,640]{1,0:T(8,128)(2,1)S(1)}, u32[]{:S(2)}, u32[]{:S(2)}) collective-permute-start(bf16[112,640]{1,0:T(8,128)(2,1)S(1)} %get-tuple-element.49), channel_id=1, source_target_pairs={{0,16},{8,24},{16,0},{24,8},{32,48},{40,56},{48,32},{56,40},{64,80... | collective-permute-start | bytes 430088 | tf_op jit(solution)/shard_map/ppermute | solution.py:24
  18.0 18.2 %collective-permute-start.5 = (bf16[96,1280]{1,0:T(8,128)(2,1)S(1)}, bf16[96,1280]{1,0:T(8,128)(2,1)S(1)}, u32[]{:S(2)}, u32[]{:S(2)}) collective-permute-start(bf16[96,1280]{1,0:T(8,128)(2,1)S(1)} %get-tuple-element.53), channel_id=1, source_target_pairs={{0,4},{1,5},{2,6},{3,7},{4,0},{5,1},{6,2},{7,3},{8,12},{9,13},{10,... | collective-permute-start | bytes 737288 | tf_op jit(solution)/shard_map/ppermute | solution.py:33
  23.9 12.4 %collective-permute-start.4 = (bf16[384,640]{1,0:T(8,128)(2,1)S(1)}, bf16[384,640]{1,0:T(8,128)(2,1)S(1)}, u32[]{:S(2)}, u32[]{:S(2)}) collective-permute-start(bf16[384,640]{1,0:T(8,128)(2,1)S(1)} %get-tuple-element.54.refs_0_), channel_id=1, source_target_pairs={{0,3},{1,0},{2,1},{3,2},{4,7},{5,4},{6,5},{7,6},{8,11},{9,8},{10,9... | collective-permute-start | bytes 1474568 | tf_op jit(solution)/shard_map/ppermute | solution.py:33
  27.5 15.3 %collective-permute-start.18 = (bf16[320,1152]{1,0:T(8,128)(2,1)S(1)}, bf16[320,1152]{1,0:T(8,128)(2,1)S(1)}, u32[]{:S(2)}, u32[]{:S(2)}) collective-permute-start(bf16[320,1152]{1,0:T(8,128)(2,1)S(1)} %shard_map.82.refs_5_), channel_id=1, source_target_pairs={{0,48},{8,56},{16,0},{24,8},{32,16},{40,24},{48,32},{56,40},{64,11... | collective-permute-start | bytes 2211848 | tf_op jit(solution)/shard_map/ppermute | solution.py:24
  29.4 16.5 %collective-permute-start.17 = (bf16[320,1152]{1,0:T(8,128)(2,1)S(1)}, bf16[320,1152]{1,0:T(8,128)(2,1)S(1)}, u32[]{:S(2)}, u32[]{:S(2)}) collective-permute-start(bf16[320,1152]{1,0:T(8,128)(2,1)S(1)} %shard_map.82.refs_5_), channel_id=1, source_target_pairs={{0,16},{8,24},{16,32},{24,40},{32,48},{40,56},{48,0},{56,8},{64,80... | collective-permute-start | bytes 2211848 | tf_op jit(solution)/shard_map/ppermute | solution.py:24
  38.9 11.8 %collective-permute-start.7 = (bf16[192,1280]{1,0:T(8,128)(2,1)S(1)}, bf16[192,1280]{1,0:T(8,128)(2,1)S(1)}, u32[]{:S(2)}, u32[]{:S(2)}) collective-permute-start(bf16[192,1280]{1,0:T(8,128)(2,1)S(1)} %pad_maximum_fusion.refs_0_), channel_id=1, source_target_pairs={{0,1},{1,2},{2,3},{3,0},{4,5},{5,6},{6,7},{7,4},{8,9},{9,10},{10,1... | collective-permute-start | bytes 1474568 | tf_op jit(solution)/shard_map/ppermute | solution.py:33
  39.1 12.4 %collective-permute-start.6 = (bf16[384,640]{1,0:T(8,128)(2,1)S(1)}, bf16[384,640]{1,0:T(8,128)(2,1)S(1)}, u32[]{:S(2)}, u32[]{:S(2)}) collective-permute-start(bf16[384,640]{1,0:T(8,128)(2,1)S(1)} %get-tuple-element.54.refs_0_), channel_id=1, source_target_pairs={{0,4},{1,5},{2,6},{3,7},{4,0},{5,1},{6,2},{7,3},{8,12},{9,13},{10,... | collective-permute-start | bytes 1474568 | tf_op jit(solution)/shard_map/ppermute | solution.py:33
  59.9 14.2 %collective-permute-start.21 = (f32[384,1152]{1,0:T(8,128)S(1)}, f32[384,1152]{1,0:T(8,128)S(1)}, u32[]{:S(2)}, u32[]{:S(2)}) collective-permute-start(f32[384,1152]{1,0:T(8,128)S(1)} %get-tuple-element.65), channel_id=1, source_target_pairs={{0,8},{8,0},{16,24},{24,16},{32,40},{40,32},{48,56},{56,48},{64,72... | collective-permute-start | bytes 5308424 | tf_op jit(solution)/shard_map/ppermute | solution.py:24
  64.5 18.5 %collective-permute-start.12 = (bf16[384,640]{1,0:T(8,128)(2,1)S(1)}, bf16[384,640]{1,0:T(8,128)(2,1)S(1)}, u32[]{:S(2)}, u32[]{:S(2)}) collective-permute-start(bf16[384,640]{1,0:T(8,128)(2,1)S(1)} %collective-permute-done.6.refs_3_), channel_id=1, source_target_pairs={{0,3},{1,0},{2,1},{3,2},{4,7},{5,4},{6,5},{7,6},{8,11},{9,8},{10,9... | collective-permute-start | bytes 1474568 | tf_op jit(solution)/shard_map/ppermute | solution.py:33
  72.4 13.7 %collective-permute-start.11 = (bf16[384,640]{1,0:T(8,128)(2,1)S(1)}, bf16[384,640]{1,0:T(8,128)(2,1)S(1)}, u32[]{:S(2)}, u32[]{:S(2)}) collective-permute-start(bf16[384,640]{1,0:T(8,128)(2,1)S(1)} %collective-permute-done.6.refs_3_), channel_id=1, source_target_pairs={{0,1},{1,2},{2,3},{3,0},{4,5},{5,6},{6,7},{7,4},{8,9},{9,10},{10,1... | collective-permute-start | bytes 1474568 | tf_op jit(solution)/shard_map/ppermute | solution.py:33
  75.7 28.8 %collective-permute-start.23 = (bf16[384,1152]{1,0:T(8,128)(2,1)S(1)}, bf16[384,1152]{1,0:T(8,128)(2,1)S(1)}, u32[]{:S(2)}, u32[]{:S(2)}) collective-permute-start(bf16[384,1152]{1,0:T(8,128)(2,1)S(1)} %get-tuple-element.66.d), channel_id=1, source_target_pairs={{0,16},{8,24},{16,0},{24,8},{32,48},{40,56},{48,32},{56,40},{64,80... | collective-permute-start | bytes 2654216 | tf_op jit(solution)/shard_map/ppermute | solution.py:24
  76.0 30.7 %collective-permute-start.29 = (bf16[384,1152]{1,0:T(8,128)(2,1)S(1)}, bf16[384,1152]{1,0:T(8,128)(2,1)S(1)}, u32[]{:S(2)}, u32[]{:S(2)}) collective-permute-start(bf16[384,1152]{1,0:T(8,128)(2,1)S(1)} %get-tuple-element.69.d), channel_id=1, source_target_pairs={{0,48},{8,56},{16,32},{24,40},{32,16},{40,24},{48,0},{56,8},{64,11... | collective-permute-start | bytes 2654216 | tf_op jit(solution)/shard_map/ppermute | solution.py:24
  78.7 21.9 %collective-permute-start.22 = (bf16[768,1152]{1,0:T(8,128)(2,1)S(1)}, bf16[768,1152]{1,0:T(8,128)(2,1)S(1)}, u32[]{:S(2)}, u32[]{:S(2)}) collective-permute-start(bf16[768,1152]{1,0:T(8,128)(2,1)S(1)} %get-tuple-element.67), channel_id=1, source_target_pairs={{0,8},{8,0},{16,24},{24,16},{32,40},{40,32},{48,56},{56,48},{64,72... | collective-permute-start | bytes 5308424 | tf_op jit(solution)/shard_map/ppermute | solution.py:24
  86.1 11.6 %collective-permute-start.24 = (bf16[384,640]{1,0:T(8,128)(2,1)S(1)}, bf16[384,640]{1,0:T(8,128)(2,1)S(1)}, u32[]{:S(2)}, u32[]{:S(2)}) collective-permute-start(bf16[384,640]{1,0:T(8,128)(2,1)S(1)} %get-tuple-element.68), channel_id=1, source_target_pairs={{0,3},{1,0},{2,1},{3,2},{4,7},{5,4},{6,5},{7,6},{8,11},{9,8},{10,9... | collective-permute-start | bytes 1474568 | tf_op jit(solution)/shard_map/ppermute | solution.py:33
  86.5 12.8 %collective-permute-start.13 = (bf16[384,640]{1,0:T(8,128)(2,1)S(1)}, bf16[384,640]{1,0:T(8,128)(2,1)S(1)}, u32[]{:S(2)}, u32[]{:S(2)}) collective-permute-start(bf16[384,640]{1,0:T(8,128)(2,1)S(1)} %get-tuple-element.57), channel_id=1, source_target_pairs={{0,1},{1,2},{2,3},{3,0},{4,5},{5,6},{6,7},{7,4},{8,9},{9,10},{10,1... | collective-permute-start | bytes 1474568 | tf_op jit(solution)/shard_map/ppermute | solution.py:33
  110.8 19.9 %collective-permute-start.26 = (bf16[336,1152]{1,0:T(8,128)(2,1)S(1)}, bf16[336,1152]{1,0:T(8,128)(2,1)S(1)}, u32[]{:S(2)}, u32[]{:S(2)}) collective-permute-start(bf16[336,1152]{1,0:T(8,128)(2,1)S(1)} %get-tuple-element.73), channel_id=1, source_target_pairs={{0,48},{8,56},{16,32},{24,40},{32,16},{40,24},{48,0},{56,8},{64,11... | collective-permute-start | bytes 2322440 | tf_op jit(solution)/shard_map/ppermute | solution.py:24
  115.7 19.4 %collective-permute-start.31 = (bf16[320,1152]{1,0:T(8,128)(2,1)S(1)}, bf16[320,1152]{1,0:T(8,128)(2,1)S(1)}, u32[]{:S(2)}, u32[]{:S(2)}) collective-permute-start(bf16[320,1152]{1,0:T(8,128)(2,1)S(1)} %get-tuple-element.83), channel_id=1, source_target_pairs={{0,16},{8,24},{16,0},{24,8},{32,48},{40,56},{48,32},{56,40},{64,80... | collective-permute-start | bytes 2211848 | tf_op jit(solution)/shard_map/ppermute | solution.py:24
  131.0 12.7 %collective-permute-start.27 = (bf16[176,1152]{1,0:T(8,128)(2,1)S(1)}, bf16[176,1152]{1,0:T(8,128)(2,1)S(1)}, u32[]{:S(2)}, u32[]{:S(2)}) collective-permute-start(bf16[176,1152]{1,0:T(8,128)(2,1)S(1)} %get-tuple-element.75), channel_id=1, source_target_pairs={{0,64},{8,72},{16,80},{24,88},{32,96},{40,104},{48,112},{56,120},{... | collective-permute-start | bytes 1216520 | tf_op jit(solution)/shard_map/ppermute | solution.py:24
  135.3 21.0 %collective-permute-start.32 = (bf16[160,1152]{1,0:T(8,128)(2,1)S(1)}, bf16[160,1152]{1,0:T(8,128)(2,1)S(1)}, u32[]{:S(2)}, u32[]{:S(2)}) collective-permute-start(bf16[160,1152]{1,0:T(8,128)(2,1)S(1)} %get-tuple-element.86), channel_id=1, source_target_pairs={{0,64},{8,72},{16,80},{24,88},{32,96},{40,104},{48,112},{56,120},{... | collective-permute-start | bytes 1105928 | tf_op jit(solution)/shard_map/ppermute | solution.py:24
  143.7 13.6 %collective-permute-start.28 = (bf16[96,1152]{1,0:T(8,128)(2,1)S(1)}, bf16[96,1152]{1,0:T(8,128)(2,1)S(1)}, u32[]{:S(2)}, u32[]{:S(2)}) collective-permute-start(bf16[96,1152]{1,0:T(8,128)(2,1)S(1)} %get-tuple-element.78), channel_id=1, source_target_pairs={{0,128},{8,136},{16,144},{24,152},{32,160},{40,168},{48,176},{56,1... | collective-permute-start | bytes 663560 | tf_op jit(solution)/shard_map/ppermute | solution.py:24
  156.3 12.2 %collective-permute-start.33 = (bf16[80,1152]{1,0:T(8,128)(2,1)S(1)}, bf16[80,1152]{1,0:T(8,128)(2,1)S(1)}, u32[]{:S(2)}, u32[]{:S(2)}) collective-permute-start(bf16[80,1152]{1,0:T(8,128)(2,1)S(1)} %get-tuple-element.88), channel_id=1, source_target_pairs={{0,128},{8,136},{16,144},{24,152},{32,160},{40,168},{48,176},{56,1... | collective-permute-start | bytes 552968 | tf_op jit(solution)/shard_map/ppermute | solution.py:24
  (16 other events, 80.8 us)
